TPU v7x, 32 devices: a whole 2x2x4 slice. The times are simulated.
32 devices in a mesh: row: 8 (over z, y), col: 4 (over x, core).
Axes of the slice: x: 2, y: 2, z: 4, core: 2. Of those that a mesh axis runs over, the one named last changes fastest.
Arguments:
- tokens: bfloat16 [8192, 768], P(('row', 'col')), may hold values from -6 to 6
- norm1_gain: float32 [768], replicated, may hold values from 0.5 to 1.5
- norm1_bias: float32 [768], replicated, may hold values from -1.25 to 1.25
- w_query: bfloat16 [768, 768], replicated, may hold values from -0.3125 to 0.3125
- b_query: float32 [768], replicated, may hold values from -1.25 to 1.25
- w_key: bfloat16 [768, 768], replicated, may hold values from -0.3125 to 0.3125
- w_value: bfloat16 [768, 768], replicated, may hold values from -0.21875 to 0.21875
- b_value: float32 [768], replicated, may hold values from -1.25 to 1.25
- w_out: bfloat16 [768, 768], replicated, may hold values from -1.75 to 1.75
- b_out: float32 [768], replicated, may hold values from -1.25 to 1.25
- norm2_gain: float32 [768], replicated, may hold values from 0.5 to 1.5
- norm2_bias: float32 [768], replicated, may hold values from -1.25 to 1.25
- w_up: bfloat16 [768, 3072], replicated, may hold values from -0.21875 to 0.21875
- b_up: float32 [3072], replicated, may hold values from -1.25 to 1.25
- w_down: bfloat16 [3072, 768], replicated, may hold values from -0.109375 to 0.109375
- b_down: float32 [768], replicated, may hold values from -1.25 to 1.25
- slide_padded_units: int32 [8], replicated, may hold values from 1 to 21, 32 in all
- padding_shortfall: int32 [8], replicated, may hold values from 0 to 255
- cotangent: bfloat16 [8192, 768], P(('row', 'col')), may hold values from -6 to 6
Outputs:
- output: bfloat16 [8192, 768], P(('row', 'col'))
- grad_tokens: float32 [8192, 768], P(('row', 'col'))
- grad_norm1_gain: float32 [768], P('row')
- grad_norm1_bias: float32 [768], P('row')
- grad_w_query: float32 [768, 768], P('row')
- grad_b_query: float32 [768], P('row')
- grad_w_key: float32 [768, 768], P('row')
- grad_w_value: float32 [768, 768], P('row')
- grad_b_value: float32 [768], P('row')
- grad_w_out: float32 [768, 768], P('row')
- grad_b_out: float32 [768], P('row')
- grad_norm2_gain: float32 [768], P('row')
- grad_norm2_bias: float32 [768], P('row')
- grad_w_up: float32 [768, 3072], P('row')
- grad_b_up: float32 [3072], P('row')
- grad_w_down: float32 [3072, 768], P('row')
- grad_b_down: float32 [768], P('row')
Inputs may be any that keep to these rules, and one draw needn't show every extreme that they name: The slides fill the sequence exactly: the slide_padded_units add up to 32, and the largest is 21. `padding_shortfall`: fewer than 256 padding tiles a slide.
All inputs are finite; a program needn't handle non-finite values.
Results may differ from a plain program's by a relative error of at most 0.017.
Values may be sent and summed in bfloat16 or wider, within the bound.
A program may use at most 256 MiB of HBM per device.

v0:
```python
import jax
import jax.numpy as jnp
from jax import lax
from jax.sharding import PartitionSpec as P

ATTENTION_HEADS = 16
HEAD_DIM = 48
DILATION_STRIDE = 16
PAD = 256


EPS = 1e-05
NEG = -1e30
head_split = 4


def product(left, right):
    return jnp.dot(left, right, preferred_element_type=jnp.float32)


def layer_norm(values, norm_gain, norm_bias):
    row_mean = jnp.mean(values, axis=-1, keepdims=True)
    centred = values - row_mean
    inverse = lax.rsqrt(jnp.mean(centred * centred, axis=-1, keepdims=True) + EPS)
    return centred * inverse * norm_gain + norm_bias


def gelu_exact(values):
    return jax.nn.gelu(values, approximate=False)


def slide_lookup_tables(slide_padded_units, padding_shortfall, positions):
    slide_ends = jnp.cumsum(slide_padded_units, dtype=jnp.int32) * PAD
    slide_starts = slide_ends - slide_padded_units * PAD
    inside = (positions[:, None] >= slide_starts[None, :]) & (
        positions[:, None] < slide_ends[None, :]
    )
    numbers = jnp.arange(slide_padded_units.shape[0], dtype=jnp.int32)
    labels = jnp.sum(jnp.where(inside, numbers[None, :], 0), axis=1, dtype=jnp.int32)
    limits = jnp.sum(
        jnp.where(inside, (slide_ends - padding_shortfall)[None, :], 0), axis=1, dtype=jnp.int32
    )
    return (labels, positions < limits)


def permitted_mask(query_positions, query_labels, key_pos, key_lab, key_valid):
    return (query_labels == key_lab) & key_valid | (query_positions == key_pos)


def log_total(scores):
    row_top = jnp.max(scores, axis=-1, keepdims=True)
    return row_top[..., 0] + jnp.log(jnp.sum(jnp.exp(scores - row_top), axis=-1))


def pick_rows(softmax_statistics, selector_portion):
    sparse_extent = selector_portion.shape[0]
    reshaped_tensor = softmax_statistics.reshape(
        softmax_statistics.shape[0], softmax_statistics.shape[1] // sparse_extent, sparse_extent
    )
    return jnp.sum(reshaped_tensor * selector_portion.T[:, None, :], axis=-1)


def merge_stats(first_total, total_b, selector_portion, chooser_bool):
    sparse_extent = selector_portion.shape[0]
    joint = jnp.logaddexp(pick_rows(first_total, selector_portion), total_b)
    reshaped_tensor = first_total.reshape(
        first_total.shape[0], first_total.shape[1] // sparse_extent, sparse_extent
    )
    full = jnp.where(chooser_bool.T[:, None, :], joint[:, :, None], reshaped_tensor).reshape(
        first_total.shape
    )
    return (joint, full)


def select_heads(row_entries, selector_float):
    sparse_extent = selector_float.shape[0]
    number_of_heads = selector_float.shape[1]
    reshaped_tensor = row_entries.reshape(
        row_entries.shape[0] // sparse_extent,
        sparse_extent,
        number_of_heads,
        row_entries.shape[1] // number_of_heads,
    )
    picked = jnp.einsum(
        "trhd,rh->thd",
        reshaped_tensor,
        selector_float.astype(row_entries.dtype),
        preferred_element_type=jnp.float32,
    )
    return picked.astype(row_entries.dtype).reshape(reshaped_tensor.shape[0], row_entries.shape[1])


def broadcast_heads(picked, selector_portion):
    number_of_heads = selector_portion.shape[1]
    grown_rows = (
        picked.reshape(picked.shape[0], 1, number_of_heads, picked.shape[1] // number_of_heads)
        * selector_portion[None, :, :, None]
    )
    return grown_rows.reshape(picked.shape[0] * selector_portion.shape[0], picked.shape[1])


def split_into_heads(row_entries, number_of_heads):
    return row_entries.reshape(
        row_entries.shape[0], number_of_heads, row_entries.shape[1] // number_of_heads
    )


def body(
    tokens,
    norm1_gain,
    norm1_bias,
    w_query,
    b_query,
    w_key,
    w_value,
    b_value,
    w_out,
    b_out,
    norm2_gain,
    norm2_bias,
    w_up,
    b_up,
    w_down,
    b_down,
    slide_padded_units,
    padding_shortfall,
    cotangent,
):
    local_count = tokens.shape[0]
    col_count = lax.axis_size("col")
    number_of_rows = lax.axis_size("row")
    segment_length = local_count * col_count
    sparse_total = segment_length * number_of_rows // DILATION_STRIDE
    local_sel = local_count // DILATION_STRIDE
    heads_per_group = ATTENTION_HEADS // head_split
    group_span_width = heads_per_group * HEAD_DIM
    score_scaling = HEAD_DIM ** (-0.5)
    first_pos = (lax.axis_index("row") * col_count + lax.axis_index("col")) * local_count
    seg_first = lax.axis_index("row") * segment_length
    head_remainder = jnp.arange(ATTENTION_HEADS, dtype=jnp.int32) % DILATION_STRIDE
    chooser_bool = head_remainder[None, :] == jnp.arange(DILATION_STRIDE, dtype=jnp.int32)[:, None]
    selector_float = chooser_bool.astype(jnp.float32)
    loc_pos = first_pos + jnp.arange(local_count, dtype=jnp.int32)
    loc_lab = slide_lookup_tables(slide_padded_units, padding_shortfall, loc_pos)[0]
    seg_pos = seg_first + jnp.arange(segment_length, dtype=jnp.int32)
    seg_lab, seg_valid = slide_lookup_tables(slide_padded_units, padding_shortfall, seg_pos)
    allow_a = permitted_mask(
        loc_pos[:, None], loc_lab[:, None], seg_pos[None, :], seg_lab[None, :], seg_valid[None, :]
    )
    sparse_positions = (
        DILATION_STRIDE * jnp.arange(sparse_total, dtype=jnp.int32)[:, None]
        + head_remainder[None, :]
    )
    sparse_labels, sparse_validity = slide_lookup_tables(
        slide_padded_units, padding_shortfall, sparse_positions.reshape(-1)
    )
    sparse_labels = sparse_labels.reshape(sparse_total, ATTENTION_HEADS)
    sparse_validity = sparse_validity.reshape(sparse_total, ATTENTION_HEADS)
    sel_pos = (
        first_pos
        + DILATION_STRIDE * jnp.arange(local_sel, dtype=jnp.int32)[:, None]
        + head_remainder[None, :]
    )
    sel_lab, sel_valid = slide_lookup_tables(
        slide_padded_units, padding_shortfall, sel_pos.reshape(-1)
    )
    sel_lab = sel_lab.reshape(local_sel, ATTENTION_HEADS)
    sel_valid = sel_valid.reshape(local_sel, ATTENTION_HEADS)
    x_rows = tokens.astype(jnp.float32)
    h_one, norm_back_one = jax.vjp(layer_norm, x_rows, norm1_gain, norm1_bias)
    a_one = h_one.astype(jnp.bfloat16)
    q_rows = (product(a_one, w_query) + b_query).astype(jnp.bfloat16)
    k_rows = product(a_one, w_key).astype(jnp.bfloat16)
    v_rows = (product(a_one, w_value) + b_value).astype(jnp.bfloat16)
    seg_keys, seg_values = (
        lax.all_gather(k_rows, "col", axis=0, tiled=True),
        lax.all_gather(v_rows, "col", axis=0, tiled=True),
    )
    k_sel = select_heads(k_rows, selector_float)
    v_sel = select_heads(v_rows, selector_float)
    sparse_keys, sparse_values = (
        lax.all_gather(k_sel, ("row", "col"), axis=0, tiled=True),
        lax.all_gather(v_sel, ("row", "col"), axis=0, tiled=True),
    )
    q_sel = select_heads(q_rows, selector_float)

    def group_mask(head_lower, head_upper):
        return permitted_mask(
            sel_pos[:, head_lower:head_upper].T[:, :, None],
            sel_lab[:, head_lower:head_upper].T[:, :, None],
            sparse_positions[:, head_lower:head_upper].T[:, None, :],
            sparse_labels[:, head_lower:head_upper].T[:, None, :],
            sparse_validity[:, head_lower:head_upper].T[:, None, :],
        )

    def group_scores(query_grp, key_grp, qdil_grp, sparse_key_group, second_allow_mask):
        scores_a = (
            jnp.einsum("ihd,jhd->hij", query_grp, key_grp, preferred_element_type=jnp.float32)
            * score_scaling
        )
        scores_a = jnp.where(allow_a[None], scores_a, NEG)
        second_scores = (
            jnp.einsum(
                "sye,fye->ysf", qdil_grp, sparse_key_group, preferred_element_type=jnp.float32
            )
            * score_scaling
        )
        second_scores = jnp.where(second_allow_mask, second_scores, NEG)
        return (scores_a, second_scores)

    joints = []
    fulls = []
    out_parts = []
    for group_index in range(head_split):
        head_lower = group_index * heads_per_group
        head_upper = head_lower + heads_per_group
        column_lower = head_lower * HEAD_DIM
        column_upper = head_upper * HEAD_DIM
        selector_portion = selector_float[:, head_lower:head_upper]
        scores_a, second_scores = group_scores(
            split_into_heads(q_rows[:, column_lower:column_upper], heads_per_group),
            split_into_heads(seg_keys[:, column_lower:column_upper], heads_per_group),
            split_into_heads(q_sel[:, column_lower:column_upper], heads_per_group),
            split_into_heads(sparse_keys[:, column_lower:column_upper], heads_per_group),
            group_mask(head_lower, head_upper),
        )
        joint, full = merge_stats(
            log_total(scores_a),
            log_total(second_scores),
            selector_portion,
            chooser_bool[:, head_lower:head_upper],
        )
        joints.append(joint)
        fulls.append(full)
        weights_a = jnp.exp(scores_a - full[:, :, None]).astype(jnp.bfloat16)
        second_weights = jnp.exp(second_scores - joint[:, :, None]).astype(jnp.bfloat16)
        out_a = jnp.einsum(
            "hij,jhd->ihd",
            weights_a,
            split_into_heads(seg_values[:, column_lower:column_upper], heads_per_group),
            preferred_element_type=jnp.float32,
        )
        second_output = jnp.einsum(
            "yxp,pyf->xyf",
            second_weights,
            split_into_heads(sparse_values[:, column_lower:column_upper], heads_per_group),
            preferred_element_type=jnp.float32,
        )
        out_parts.append(
            out_a.reshape(local_count, group_span_width)
            + broadcast_heads(second_output.reshape(local_sel, group_span_width), selector_portion)
        )
    attended = jnp.concatenate(out_parts, axis=1).astype(jnp.bfloat16)
    y_one = x_rows + product(attended, w_out) + b_out
    h_two, norm_back_two = jax.vjp(layer_norm, y_one, norm2_gain, norm2_bias)
    a_two = h_two.astype(jnp.bfloat16)
    up_rows = product(a_two, w_up) + b_up
    hidden_f, gelu_back = jax.vjp(gelu_exact, up_rows)
    hidden = hidden_f.astype(jnp.bfloat16)
    output_rows = (y_one + product(hidden, w_down) + b_down).astype(jnp.bfloat16)
    cot_f = cotangent.astype(jnp.float32)
    g_w_down = product(hidden.T, cotangent)
    g_b_down = jnp.sum(cot_f, axis=0)
    d_up = gelu_back(product(cotangent, w_down.T))[0].astype(jnp.bfloat16)
    g_w_up = product(a_two.T, d_up)
    g_b_up = jnp.sum(d_up.astype(jnp.float32), axis=0)
    d_ytwo, g_norm2_gain, g_norm2_bias = norm_back_two(product(d_up, w_up.T))
    d_yone = d_ytwo + cot_f
    d_branch = d_yone.astype(jnp.bfloat16)
    g_w_out = product(attended.T, d_branch)
    g_b_out = jnp.sum(d_branch.astype(jnp.float32), axis=0)
    d_att = product(d_branch, w_out.T).astype(jnp.bfloat16)
    d_att_sel = select_heads(d_att, selector_float)
    dq_parts = []
    dka_parts = []
    dva_parts = []
    dkb_parts = []
    dvb_parts = []
    rowj_parts = []
    for group_index in range(head_split):
        head_lower = group_index * heads_per_group
        head_upper = head_lower + heads_per_group
        column_lower = head_lower * HEAD_DIM
        column_upper = head_upper * HEAD_DIM
        selector_portion = selector_float[:, head_lower:head_upper]
        query_grp = split_into_heads(q_rows[:, column_lower:column_upper], heads_per_group)
        key_grp = split_into_heads(seg_keys[:, column_lower:column_upper], heads_per_group)
        value_grp = split_into_heads(seg_values[:, column_lower:column_upper], heads_per_group)
        qdil_grp = split_into_heads(q_sel[:, column_lower:column_upper], heads_per_group)
        sparse_key_group = split_into_heads(
            sparse_keys[:, column_lower:column_upper], heads_per_group
        )
        sparse_value_group = split_into_heads(
            sparse_values[:, column_lower:column_upper], heads_per_group
        )
        dout_grp = split_into_heads(d_att[:, column_lower:column_upper], heads_per_group)
        ddil_grp = split_into_heads(d_att_sel[:, column_lower:column_upper], heads_per_group)
        scores_a, second_scores = group_scores(
            query_grp, key_grp, qdil_grp, sparse_key_group, group_mask(head_lower, head_upper)
        )
        weights_a = jnp.exp(scores_a - fulls[group_index][:, :, None])
        second_weights = jnp.exp(second_scores - joints[group_index][:, :, None])
        dw_a = jnp.einsum("ihd,jhd->hij", dout_grp, value_grp, preferred_element_type=jnp.float32)
        dw_b = jnp.einsum(
            "sye,fye->ysf", ddil_grp, sparse_value_group, preferred_element_type=jnp.float32
        )
        row_a = jnp.sum(weights_a * dw_a, axis=-1)
        row_b = jnp.sum(second_weights * dw_b, axis=-1)
        row_full = (
            row_a.reshape(heads_per_group, local_sel, DILATION_STRIDE)
            + row_b[:, :, None] * selector_portion.T[:, None, :]
        ).reshape(heads_per_group, local_count)
        row_joint = pick_rows(row_a, selector_portion) + row_b
        rowj_parts.append(row_joint)
        ds_a = (weights_a * (dw_a - row_full[:, :, None])).astype(jnp.bfloat16)
        ds_b = (second_weights * (dw_b - row_joint[:, :, None])).astype(jnp.bfloat16)
        dq_a = (
            jnp.einsum("hij,jhd->ihd", ds_a, key_grp, preferred_element_type=jnp.float32)
            * score_scaling
        )
        dq_b = (
            jnp.einsum("yxp,pyf->xyf", ds_b, sparse_key_group, preferred_element_type=jnp.float32)
            * score_scaling
        )
        dq_parts.append(
            dq_a.reshape(local_count, group_span_width)
            + broadcast_heads(dq_b.reshape(local_sel, group_span_width), selector_portion)
        )
        dka_parts.append(
            (
                jnp.einsum("hij,ihd->jhd", ds_a, query_grp, preferred_element_type=jnp.float32)
                * score_scaling
            ).reshape(segment_length, group_span_width)
        )
        dva_parts.append(
            jnp.einsum(
                "hij,ihd->jhd",
                weights_a.astype(jnp.bfloat16),
                dout_grp,
                preferred_element_type=jnp.float32,
            ).reshape(segment_length, group_span_width)
        )
        dkb_parts.append(
            (
                jnp.einsum("htu,thd->uhd", ds_b, qdil_grp, preferred_element_type=jnp.float32)
                * score_scaling
            ).reshape(sparse_total, group_span_width)
        )
        dvb_parts.append(
            jnp.einsum(
                "htu,thd->uhd",
                second_weights.astype(jnp.bfloat16),
                ddil_grp,
                preferred_element_type=jnp.float32,
            ).reshape(sparse_total, group_span_width)
        )
    segment_key_gradient, segment_value_gradient = (
        lax.psum_scatter(
            jnp.concatenate(dka_parts, axis=1).astype(jnp.bfloat16),
            "col",
            scatter_dimension=0,
            tiled=True,
        ).astype(jnp.float32),
        lax.psum_scatter(
            jnp.concatenate(dva_parts, axis=1).astype(jnp.bfloat16),
            "col",
            scatter_dimension=0,
            tiled=True,
        ).astype(jnp.float32),
    )
    sparse_key_gradient, sparse_value_gradient = (
        lax.psum_scatter(
            jnp.concatenate(dkb_parts, axis=1), ("row", "col"), scatter_dimension=0, tiled=True
        ),
        lax.psum_scatter(
            jnp.concatenate(dvb_parts, axis=1), ("row", "col"), scatter_dimension=0, tiled=True
        ),
    )
    dq_low = jnp.concatenate(dq_parts, axis=1).astype(jnp.bfloat16)
    key_gradient_lower = (
        segment_key_gradient + broadcast_heads(sparse_key_gradient, selector_float)
    ).astype(jnp.bfloat16)
    value_gradient_lower = (
        segment_value_gradient + broadcast_heads(sparse_value_gradient, selector_float)
    ).astype(jnp.bfloat16)
    g_w_query = product(a_one.T, dq_low)
    g_b_query = jnp.sum(dq_low.astype(jnp.float32), axis=0)
    g_w_key = product(a_one.T, key_gradient_lower)
    g_w_value = product(a_one.T, value_gradient_lower)
    g_b_value = jnp.sum(value_gradient_lower.astype(jnp.float32), axis=0)
    d_aone = (
        product(dq_low, w_query.T)
        + product(key_gradient_lower, w_key.T)
        + product(value_gradient_lower, w_value.T)
    )
    d_xnorm, g_norm1_gain, g_norm1_bias = norm_back_one(d_aone)
    grad_rows = d_yone + d_xnorm
    (
        part_gone,
        part_bone,
        part_wq,
        part_bq,
        part_wk,
        part_wv,
        part_bv,
        part_wo,
        part_bo,
        part_gtwo,
        part_btwo,
        part_wup,
        part_bup,
        part_wdown,
        part_bdown,
    ) = (
        lax.psum_scatter(g_norm1_gain, "row", scatter_dimension=0, tiled=True),
        lax.psum_scatter(g_norm1_bias, "row", scatter_dimension=0, tiled=True),
        lax.psum_scatter(g_w_query, "row", scatter_dimension=0, tiled=True),
        lax.psum_scatter(g_b_query, "row", scatter_dimension=0, tiled=True),
        lax.psum_scatter(g_w_key, "row", scatter_dimension=0, tiled=True),
        lax.psum_scatter(g_w_value, "row", scatter_dimension=0, tiled=True),
        lax.psum_scatter(g_b_value, "row", scatter_dimension=0, tiled=True),
        lax.psum_scatter(g_w_out, "row", scatter_dimension=0, tiled=True),
        lax.psum_scatter(g_b_out, "row", scatter_dimension=0, tiled=True),
        lax.psum_scatter(g_norm2_gain, "row", scatter_dimension=0, tiled=True),
        lax.psum_scatter(g_norm2_bias, "row", scatter_dimension=0, tiled=True),
        lax.psum_scatter(g_w_up, "row", scatter_dimension=0, tiled=True),
        lax.psum_scatter(g_b_up, "row", scatter_dimension=0, tiled=True),
        lax.psum_scatter(g_w_down, "row", scatter_dimension=0, tiled=True),
        lax.psum_scatter(g_b_down, "row", scatter_dimension=0, tiled=True),
    )
    totals = (
        lax.psum(part_gone.astype(jnp.bfloat16), "col").astype(jnp.float32),
        lax.psum(part_bone.astype(jnp.bfloat16), "col").astype(jnp.float32),
        lax.psum(part_wq.astype(jnp.bfloat16), "col").astype(jnp.float32),
        lax.psum(part_bq.astype(jnp.bfloat16), "col").astype(jnp.float32),
        lax.psum(part_wk.astype(jnp.bfloat16), "col").astype(jnp.float32),
        lax.psum(part_wv.astype(jnp.bfloat16), "col").astype(jnp.float32),
        lax.psum(part_bv.astype(jnp.bfloat16), "col").astype(jnp.float32),
        lax.psum(part_wo.astype(jnp.bfloat16), "col").astype(jnp.float32),
        lax.psum(part_bo.astype(jnp.bfloat16), "col").astype(jnp.float32),
        lax.psum(part_gtwo.astype(jnp.bfloat16), "col").astype(jnp.float32),
        lax.psum(part_btwo.astype(jnp.bfloat16), "col").astype(jnp.float32),
        lax.psum(part_wup.astype(jnp.bfloat16), "col").astype(jnp.float32),
        lax.psum(part_bup.astype(jnp.bfloat16), "col").astype(jnp.float32),
        lax.psum(part_wdown.astype(jnp.bfloat16), "col").astype(jnp.float32),
        lax.psum(part_bdown.astype(jnp.bfloat16), "col").astype(jnp.float32),
    )
    return (output_rows, grad_rows) + tuple(totals)


def solution(mesh):
    placed = (
        P(("row", "col"), None),
        P(),
        P(),
        P(),
        P(),
        P(),
        P(),
        P(),
        P(),
        P(),
        P(),
        P(),
        P(),
        P(),
        P(),
        P(),
        P(),
        P(),
        P(("row", "col"), None),
    )
    return jax.shard_map(
        body,
        mesh=mesh,
        in_specs=placed,
        out_specs=(
            P(("row", "col"), None),
            P(("row", "col"), None),
            P("row"),
            P("row"),
            P("row", None),
            P("row"),
            P("row", None),
            P("row", None),
            P("row"),
            P("row", None),
            P("row"),
            P("row"),
            P("row"),
            P("row", None),
            P("row"),
            P("row", None),
            P("row"),
        ),
        check_vma=False,
    )
```

profile of v0, /device:TPU:0, one launch (start us, length us, event | category | flops | bytes accessed | tf_op | source)
XLA Modules:
  0.0 1223.2 jit_solution(15709554329634494501)
XLA Ops:
  72.3 45.3 %all_gather.15 = bf16[512,768]{1,0:T(8,128)(2,1)S(1)} all-gather(bf16[16,768]{1,0:T(8,128)(2,1)S(1)} %reshape.906), channel_id=1, replica_groups=mesh['row'=8,'col'=4] {'row','col'}, dimensions={0}, use_global_device_ids=true | all-gather | bytes 811008 | tf_op jit(solution)/shard_map/all_gather | solution.py:183
  123.6 39.0 %all_gather.14 = bf16[512,768]{1,0:T(8,128)(2,1)S(1)} all-gather(bf16[16,768]{1,0:T(8,128)(2,1)S(1)} %reshape.902), channel_id=1, replica_groups=mesh['row'=8,'col'=4] {'row','col'}, dimensions={0}, use_global_device_ids=true | all-gather | bytes 811008 | tf_op jit(solution)/shard_map/all_gather | solution.py:182
  191.5 3.4 exponential_reduce_fusion.3
  195.1 3.6 exponential_reduce_fusion.2
  201.4 3.5 fusion.111
  205.8 3.4 fusion.102
  210.1 3.4 fusion.108
  226.9 4.0 convolution_add_fusion
  230.9 10.8 convert_reduce_fusion
  280.7 4.5 fusion.146
  289.1 10.5 multiply_reduce_fusion.3
  323.5 15.0 %multiply_convert_fusion.3 = (bf16[4,256,1024]{2,1,0:T(8,128)(2,1)S(1)}, bf16[4,256,1024]{2,1,0:T(8,128)(2,1)}, bf16[4,256,1024]{2,1,0:T(8,128)(2,1)}, bf16[4,256,1024]{2,1,0:T(8,128)(2,1)}) fusion(f32[4,256,1024]{2,1,0:T(8,128)} %get-tuple-element.173, f32[4,256,1024]{2,1,0:T(8,128)} %copy-done.5, f32[4,256]{1,0:T(4,128)S(1)} %add.621, ...), kind=kLoop, calls=%fused_computation.7 | loop fusion | flops 25165824 | bytes 42237952 | tf_op jit(solution)/shard_map/convert_element_type | solution.py:315
  360.5 3.4 convolution_convert_fusion.3
  365.0 3.4 convolution_convert_fusion.2
  369.4 3.4 convolution_convert_fusion
  373.9 3.4 convolution_convert_fusion.1
  378.3 3.4 pad_maximum_fusion.2
  415.2 59.1 %reduce-scatter.31.cloned.1.call-done = f32[16,768]{1,0:T(8,128)} async-done(((f32[512,768]{1,0:T(8,128)}), f32[16,768]{1,0:T(8,128)}) %reduce-scatter.31.cloned.1.call-update) | async-done | bytes 49168
  480.4 23.5 %reduce-scatter.15.cloned.1.call-done = bf16[256,768]{1,0:T(8,128)(2,1)} async-done(((bf16[1024,768]{1,0:T(8,128)(2,1)}), bf16[256,768]{1,0:T(8,128)(2,1)}) %reduce-scatter.15.cloned.1.call-update) | async-done | bytes 393232 | tf_op jit(solution)/shard_map/reduce_scatter | solution.py:358
  510.1 24.5 %reduce-scatter.17.cloned.1.call-done = bf16[256,768]{1,0:T(8,128)(2,1)} async-done(((bf16[1024,768]{1,0:T(8,128)(2,1)}), bf16[256,768]{1,0:T(8,128)(2,1)}) %reduce-scatter.17.cloned.1.call-update) | async-done | bytes 393232 | tf_op jit(solution)/shard_map/reduce_scatter | solution.py:364
  538.9 6.9 fusion.114
  545.9 3.4 multiply_convert_fusion.4
  550.5 5.0 fusion.147
  561.4 5.1 fusion.16
  568.1 38.9 %reduce-scatter.25.cloned.1.call-done = f32[96,768]{1,0:T(8,128)} async-done(((f32[768,768]{1,0:T(8,128)}), f32[96,768]{1,0:T(8,128)}) %reduce-scatter.25.cloned.1.call-update) | async-done | bytes 294928 | tf_op jit(solution)/shard_map/reduce_scatter | solution.py:422
  608.7 69.9 %reduce-scatter.19.cloned.1.call-done = f32[96,768]{1,0:T(8,128)} async-done(((f32[768,768]{1,0:T(8,128)}), f32[96,768]{1,0:T(8,128)}) %reduce-scatter.19.cloned.1.call-update) | async-done | bytes 294928 | tf_op jit(solution)/shard_map/reduce_scatter | solution.py:417
  680.2 69.9 %reduce-scatter.21.cloned.1.call-done = f32[96,768]{1,0:T(8,128)} async-done(((f32[768,768]{1,0:T(8,128)}), f32[96,768]{1,0:T(8,128)}) %reduce-scatter.21.cloned.1.call-update) | async-done | bytes 294928 | tf_op jit(solution)/shard_map/reduce_scatter | solution.py:419
  751.8 69.9 %reduce-scatter.23.cloned.1.call-done = f32[96,768]{1,0:T(8,128)} async-done(((f32[768,768]{1,0:T(8,128)}), f32[96,768]{1,0:T(8,128)}) %reduce-scatter.23.cloned.1.call-update) | async-done | bytes 294928 | tf_op jit(solution)/shard_map/reduce_scatter | solution.py:420
  823.3 164.5 %reduce-scatter.27.cloned.1.call-done = f32[96,3072]{1,0:T(8,128)} async-done(((f32[768,3072]{1,0:T(8,128)}), f32[96,3072]{1,0:T(8,128)}) %reduce-scatter.27.cloned.1.call-update) | async-done | bytes 1179664 | tf_op jit(solution)/shard_map/reduce_scatter | solution.py:426
  990.0 163.9 %reduce-scatter.29.cloned.1.call-done = f32[384,768]{1,0:T(8,128)} async-done(((f32[3072,768]{1,0:T(8,128)}), f32[384,768]{1,0:T(8,128)}) %reduce-scatter.29.cloned.1.call-update) | async-done | bytes 1179664 | tf_op jit(solution)/shard_map/reduce_scatter | solution.py:428
  1158.9 35.6 %all-reduce.9 = (bf16[768]{0:T(1024)(128)(2,1)S(1)}, bf16[768]{0:T(1024)(128)(2,1)S(1)}, bf16[768]{0:T(1024)(128)(2,1)S(1)}, bf16[768]{0:T(1024)(128)(2,1)S(1)},...) all-reduce(f32[768]{0:T(1024)S(1)} %get-tuple-element.19, ...), channel_id=6, replica_groups=mesh['row'=8,'col'=4] {'row'}, use_global_device_ids=true, to_apply=%region_52.53.clone | all-reduce | flops 9216 | bytes 55296
  1195.2 6.4 all-reduce.10
  (738 shorter events, 294.4 us)
Async XLA Ops:
  7.2 161.6 %all-gather.3.cloned.1.call-start = ((), (), s32[]{:S(2)}) async-start(), calls=%async_computation.10 | async-start | bytes 1966080 | tf_op jit(solution)/shard_map/all_gather | solution.py:177
  12.2 166.8 %all-gather.5.cloned.1.call-start = ((), (), s32[]{:S(2)}) async-start(), calls=%async_computation.11 | async-start | bytes 1966080 | tf_op jit(solution)/shard_map/all_gather | solution.py:176
  14.9 399.2 %reduce-scatter.33.cloned.1.call-start = ((), (), s32[]{:S(2)}) async-start(), calls=%async_computation.21 | async-start | bytes 1622016
  35.0 184.4 %copy-start.83 = (f32[16,4]{1,0:T(8,128)}, f32[16,4]{1,0:T(8,128)S(1)}, u32[]{:S(2)}) copy-start(f32[16,4]{1,0:T(8,128)S(1)} %get-tuple-element.133) | copy-start | bytes 772
  35.0 184.8 %copy-start.85 = (f32[16,4]{1,0:T(8,128)}, f32[16,4]{1,0:T(8,128)S(1)}, u32[]{:S(2)}) copy-start(f32[16,4]{1,0:T(8,128)S(1)} %get-tuple-element.132) | copy-start | bytes 772
  43.8 144.5 %copy-start.54 = (bf16[256,192]{0,1:T(8,128)(2,1)}, bf16[256,192]{0,1:T(8,128)(2,1)S(1)}, u32[]{:S(2)}) copy-start(bf16[256,192]{0,1:T(8,128)(2,1)S(1)} %copy.302) | copy-start | bytes 294916
  123.3 42.4 %copy-start.100 = (bf16[16,4,48]{2,1,0:T(4,128)(2,1)S(1)}, bf16[16,4,48]{2,1,0:T(4,128)(2,1)}, u32[]{:S(2)}) copy-start(bf16[16,4,48]{2,1,0:T(4,128)(2,1)} %reshape.918) | copy-start | bytes 18436
  123.3 42.4 %copy-start.145 = (s32[4,512]{1,0:T(4,128)S(1)}, s32[4,512]{1,0:T(4,128)}, u32[]{:S(2)}) copy-start(s32[4,512]{1,0:T(4,128)} %copy.292) | copy-start | bytes 24580
  123.3 42.4 %copy-start.146 = (s32[4,512]{1,0:T(4,128)S(1)}, s32[4,512]{1,0:T(4,128)}, u32[]{:S(2)}) copy-start(s32[4,512]{1,0:T(4,128)} %copy.295) | copy-start | bytes 24580
  123.3 42.4 %copy-start.163 = (s32[4,16]{1,0:T(4,128)S(1)}, s32[4,16]{1,0:T(4,128)}, u32[]{:S(2)}) copy-start(s32[4,16]{1,0:T(4,128)} %copy.291) | copy-start | bytes 772
  123.5 43.2 %copy-start.101 = (bf16[16,4,48]{2,1,0:T(4,128)(2,1)S(1)}, bf16[16,4,48]{2,1,0:T(4,128)(2,1)}, u32[]{:S(2)}) copy-start(bf16[16,4,48]{2,1,0:T(4,128)(2,1)} %reshape.911) | copy-start | bytes 18436
  123.5 43.2 %copy-start.143 = (s32[4,512]{1,0:T(4,128)S(1)}, s32[4,512]{1,0:T(4,128)}, u32[]{:S(2)}) copy-start(s32[4,512]{1,0:T(4,128)} %copy.277) | copy-start | bytes 24580
  123.5 43.2 %copy-start.144 = (s32[4,512]{1,0:T(4,128)S(1)}, s32[4,512]{1,0:T(4,128)}, u32[]{:S(2)}) copy-start(s32[4,512]{1,0:T(4,128)} %copy.280) | copy-start | bytes 24580
  123.6 43.2 %copy-start.162 = (s32[4,16]{1,0:T(4,128)S(1)}, s32[4,16]{1,0:T(4,128)}, u32[]{:S(2)}) copy-start(s32[4,16]{1,0:T(4,128)} %copy.276) | copy-start | bytes 772
  123.6 43.2 %copy-start.164 = (s32[4,16]{1,0:T(4,128)S(1)}, s32[4,16]{1,0:T(4,128)}, u32[]{:S(2)}) copy-start(s32[4,16]{1,0:T(4,128)} %copy.279) | copy-start | bytes 772
  123.6 43.2 %copy-start.170 = (pred[4,512]{1,0:T(4,128)(4,1)S(1)}, pred[4,512]{1,0:T(4,128)(4,1)}, u32[]{:S(2)}) copy-start(pred[4,512]{1,0:T(4,128)(4,1)} %copy.278) | copy-start | bytes 6148
  199.0 58.6 %copy-start.89 = (f32[4,16]{1,0:T(4,128)}, f32[4,16]{1,0:T(4,128)S(1)}, u32[]{:S(2)}) copy-start(f32[4,16]{1,0:T(4,128)S(1)} %add_select_fusion.1) | copy-start | bytes 772
  199.6 53.5 %copy-start.90 = (f32[4,16]{1,0:T(4,128)}, f32[4,16]{1,0:T(4,128)S(1)}, u32[]{:S(2)}) copy-start(f32[4,16]{1,0:T(4,128)S(1)} %add_select_fusion.2) | copy-start | bytes 772
  200.3 61.7 %copy-start.91 = (f32[4,16]{1,0:T(4,128)}, f32[4,16]{1,0:T(4,128)S(1)}, u32[]{:S(2)}) copy-start(f32[4,16]{1,0:T(4,128)S(1)} %add_select_fusion) | copy-start | bytes 772
  200.9 64.5 %copy-start.92 = (f32[4,16]{1,0:T(4,128)}, f32[4,16]{1,0:T(4,128)S(1)}, u32[]{:S(2)}) copy-start(f32[4,16]{1,0:T(4,128)S(1)} %add_select_fusion.3) | copy-start | bytes 772
  278.7 195.7 %reduce-scatter.31.cloned.1.call-start = ((), (), s32[]{:S(2)}) async-start(), calls=%async_computation.20 | async-start | bytes 1622016
  323.4 180.5 %reduce-scatter.15.cloned.1.call-start = ((), (), s32[]{:S(2)}) async-start(), calls=%async_computation.12 | async-start | bytes 1966080 | tf_op jit(solution)/shard_map/reduce_scatter | solution.py:358
  360.3 174.4 %reduce-scatter.17.cloned.1.call-start = ((), (), s32[]{:S(2)}) async-start(), calls=%async_computation.13 | async-start | bytes 1966080 | tf_op jit(solution)/shard_map/reduce_scatter | solution.py:364
  381.7 225.3 %reduce-scatter.25.cloned.1.call-start = ((), (), s32[]{:S(2)}) async-start(), calls=%async_computation.17 | async-start | bytes 2654208 | tf_op jit(solution)/shard_map/reduce_scatter | solution.py:422
  385.2 293.4 %reduce-scatter.19.cloned.1.call-start = ((), (), s32[]{:S(2)}) async-start(), calls=%async_computation.14 | async-start | bytes 2654208 | tf_op jit(solution)/shard_map/reduce_scatter | solution.py:417
  413.7 336.4 %reduce-scatter.21.cloned.1.call-start = ((), (), s32[]{:S(2)}) async-start(), calls=%async_computation.15 | async-start | bytes 2654208 | tf_op jit(solution)/shard_map/reduce_scatter | solution.py:419
  507.1 314.7 %reduce-scatter.23.cloned.1.call-start = ((), (), s32[]{:S(2)}) async-start(), calls=%async_computation.16 | async-start | bytes 2654208 | tf_op jit(solution)/shard_map/reduce_scatter | solution.py:420
  538.9 449.0 %reduce-scatter.27.cloned.1.call-start = ((), (), s32[]{:S(2)}) async-start(), calls=%async_computation.18 | async-start | bytes 10616832 | tf_op jit(solution)/shard_map/reduce_scatter | solution.py:426
  545.9 608.0 %reduce-scatter.29.cloned.1.call-start = ((), (), s32[]{:S(2)}) async-start(), calls=%async_computation.19 | async-start | bytes 10616832 | tf_op jit(solution)/shard_map/reduce_scatter | solution.py:428
  555.6 650.7 %all-reduce.14.cloned.1.call-start = ((), (), s32[]{:S(2)}) async-start(), calls=%async_computation.22 | async-start | bytes 3538944 | tf_op jit(solution)/shard_map/psum | solution.py:434
  680.2 475.8 %copy-start.125 = (f32[256]{0:T(256)S(1)}, f32[256]{0:T(256)}, u32[]{:S(2)}) copy-start(f32[256]{0:T(256)} %copy-done.124) | copy-start | bytes 3076
  823.3 333.2 %copy-start.127 = (f32[256]{0:T(256)S(1)}, f32[256]{0:T(256)}, u32[]{:S(2)}) copy-start(f32[256]{0:T(256)} %copy-done.126) | copy-start | bytes 3076
  (166 other events, 1690.5 us)
Sparse Core Ops, SparseCore 0:
  12.3 22.3 all-gather.2
  36.2 19.6 all-gather.4
  278.8 94.4 reduce-scatter.32
  378.3 95.9 reduce-scatter.30
  476.7 27.1 reduce-scatter.14
  506.5 28.1 reduce-scatter.16
  538.2 68.8 reduce-scatter.24
  610.5 68.0 reduce-scatter.18
  682.1 68.0 reduce-scatter.20
  753.5 68.1 reduce-scatter.22
  825.3 162.5 reduce-scatter.26
  991.3 162.5 reduce-scatter.28
  1157.8 46.3 all-reduce.13
where the time goes:
time: 1240 us; the launch traced here: 1220 us
  waiting for transfers between devices  684 us (55%)
  matrix products  159 us (13%)
  local copies, waits for them, and re-layouts  134 us (11%)
  blocking collectives  126 us (10%)
  other arithmetic  98.8 us (8%)
  between operations  18.6 us (2%)
    reduce_scatter x1, waiting for transfers between devices, body(): lax.psum_scatter(g_w_up, 'row', scatter_dimension=0, tiled=True)  165 us
    reduce_scatter x1, waiting for transfers between devices, body(): lax.psum_scatter(g_w_down, 'row', scatter_dimension=0, tiled=True)  164 us
    reduce_scatter x1, waiting for transfers between devices, body(): lax.psum_scatter(g_w_key, 'row', scatter_dimension=0, tiled=True)  69.9 us
    reduce_scatter x1, waiting for transfers between devices, body(): lax.psum_scatter(g_w_query, 'row', scatter_dimension=0, tiled=True)  69.9 us
    reduce_scatter x1, waiting for transfers between devices, body(): lax.psum_scatter(g_w_value, 'row', scatter_dimension=0, tiled=True)  69.9 us
    unnamed x15, waiting for transfers between devices  59.3 us
    dot_general x18, matrix products, product(): return jnp.dot(left, right, preferred_element_type=jnp.float32)  57.1 us
    all_gather x1, blocking collectives, body(): lax.all_gather(v_sel, ('row', 'col'), axis=0, tiled=True)  45.3 us
  transfers between devices with their start and end apart: 13, of which 9 were waited for; matrix products, arithmetic and copies ran while one was open for 22% of the time, Pallas kernels for 0%

commit v1 on v0

v1 whole, which is shorter than its diff:
```python
import functools

import jax
import jax.numpy as jnp
from jax import lax
from jax.experimental import pallas as pl
from jax.experimental.pallas import tpu as pltpu
from jax.sharding import PartitionSpec as P

HEADS = 16
HEAD_DIM = 48
SLOT = 64
STRIDE = 16
PAD = 256
COLS = 4
LOCAL_HEADS = HEADS // COLS
EPS = 1e-05
NEG = -1e30
SCALE = HEAD_DIM**-0.5
SCALE2 = SCALE * 1.4426950408889634
MESH = pl.DeviceIdType.MESH
BF16 = jnp.bfloat16
F32 = jnp.float32
UNITS = (768, 768, 256, 640)
OFFSETS = (0, 768, 1536, 1792)
WIDTH = 2432


def nn(left, right):
    return jnp.dot(left, right, preferred_element_type=F32)


def nt(left, right):
    return lax.dot_general(left, right, (((1,), (1,)), ((), ())), preferred_element_type=F32)


def tn(left, right):
    return lax.dot_general(left, right, (((0,), (0,)), ((), ())), preferred_element_type=F32)


def iota(shape, dim):
    return lax.broadcasted_iota(jnp.int32, shape, dim)


def onehot(test):
    return jnp.where(test, 1.0, 0.0).astype(BF16)


def moved(values, chooser, parts=3):
    total = None
    for i in range(parts):
        low = values.astype(BF16)
        term = nn(low, chooser)
        total = term if total is None else total + term
        if i < parts - 1:
            values = values - low.astype(F32)
    return total


def normalise(x):
    centred = x - jnp.mean(x, axis=-1, keepdims=True)
    inverse = lax.rsqrt(jnp.mean(centred * centred, axis=-1, keepdims=True) + EPS)
    return centred * inverse, inverse


def norm_back(grad, unit, inverse, gain):
    scaled = grad * gain
    mean_one = jnp.mean(scaled, axis=-1, keepdims=True)
    mean_two = jnp.mean(scaled * unit, axis=-1, keepdims=True)
    return inverse * (scaled - mean_one - unit * mean_two)


def gelu_parts(u):
    z = jnp.abs(u) * 0.7071067811865476
    e = jnp.exp(-z * z)
    t = 1.0 / (1.0 + 0.3275911 * z)
    poly = t * (0.254829592 + t * (-0.284496736 + t * (1.421413741 + t * (-1.453152027 + t * 1.061405429))))
    tail = 0.5 * poly * e
    phi = jnp.where(u >= 0, 1.0 - tail, tail)
    return u * phi, phi + u * e * 0.3989422804014327


def colsum(x):
    return jnp.sum(x, axis=0, keepdims=True)


def layer(
    rows_n, slides_n, stop,
    slide_units, shortfall, par, tok_h, cot_h, wq_h, wk_h, wv_h, wo_h, wup_h, wdn_h, wdq_h,
    out_h, gt_h, gath_h, vec_h, p_h,
    wup, wdn, wqkv, wupq, wdq, wop,
    tok, gb, a1, a2, drb,
    qf, qrow, kaug, vaug, qtm, kt, vta, sdr,
    pbuf, sref, dsb, oa, att,
    y1, acc, da2, dqt, dqr,
    slab0, slab1, slab2, ra0, ra1, ra2, ra3, rb0, rb1, rb2, rb3, gath,
    kvs, qsel, wb, dqb, dkvr,
    vec, vpair, vrow, vcol, bupq, bqkv,
    lsem, gss, gsr, sps, spr, bss, bsr, u1s, u1r, u2s, u2r, ucs, ucr, ats, atr, vss, vsr, vcs, vcr, psem,
):
    row_a = rows_n // 2
    share = 768 // rows_n
    r = lax.axis_index("row")
    c = lax.axis_index("col")
    sib = c + 1 - 2 * (c % 2)
    across = (c + 2) % COLS
    diag = (sib + 2) % COLS
    ra, rbit = r // 2, r % 2
    recv_a, recv_b = (ra0, ra1, ra2, ra3), (rb0, rb1, rb2, rb3)
    slabs = (slab0, slab1, slab2, slab0.at[:, :, :, pl.ds(0, UNITS[3])])
    key_count = rows_n * 64

    def local(src, dst, i):
        return pltpu.make_async_copy(src, dst, lsem.at[i])

    in_tok = local(tok_h, tok.at[c], 0)
    in_cot = local(cot_h, gb.at[c], 1)
    in_qkv = [local(h, wup.at[:, pl.ds(768 * i, 768)], 2 + i) for i, h in enumerate((wq_h, wk_h, wv_h))]
    in_up = local(wup_h, wup, 5)
    in_dn = local(wdn_h, wdn, 6)
    in_dq = local(wdq_h, wdq, 7)
    in_wo = [
        local(wo_h.at[pl.ds(192 * s + 48 * h, 48), :], wop.at[s, pl.ds(64 * h, 48), :], 8 + 4 * s + h)
        for s in range(4)
        for h in range(4)
    ]
    in_tok.start()
    in_cot.start()
    for d in in_qkv:
        d.start()

    bar = pltpu.get_barrier_semaphore()
    for j in range(1, COLS):
        pl.semaphore_signal(bar, inc=1, device_id=(r, (c + j) % COLS), device_id_type=MESH)

    def greet(j, carry):
        pl.semaphore_signal(bar, inc=1, device_id=((r + j) % rows_n, c), device_id_type=MESH)
        return carry

    lax.fori_loop(1, rows_n, greet, 0)
    in_dq.start()
    for d in in_wo:
        d.start()
    in_dn.start()
    pl.semaphore_wait(bar, COLS - 1 + rows_n - 1)

    def remote(src, dst, send, recv, dev):
        return pltpu.make_async_remote_copy(
            src_ref=src, dst_ref=dst, send_sem=send, recv_sem=recv, device_id=dev, device_id_type=MESH
        )

    class Gather:
        def __init__(self, n, slot):
            self.near = remote(slot(c), slot(c), gss.at[n, 0], gsr.at[n, 0], (r, sib))
            self.far = remote(slot(c), slot(c), gss.at[n, 1], gsr.at[n, 1], (r, across))
            self.hand = remote(slot(across), slot(across), gss.at[n, 2], gsr.at[n, 2], (r, sib))

        def start(self):
            self.far.start()
            self.near.start()

        def forward(self):
            self.far.wait_recv()
            self.hand.start()

        def drain(self):
            self.near.wait_send()
            self.far.wait_send()
            self.hand.wait_send()

    g_tok = Gather(0, lambda i: tok.at[i])
    g_cot = Gather(1, lambda i: gb.at[i])
    g_att = [Gather(2 + p, lambda i, p=p: att.at[i, p]) for p in range(2)]
    g_dr = Gather(4, lambda i: drb.at[i])

    in_tok.wait()
    g_tok.start()
    in_cot.wait()
    g_cot.start()

    ends, lims = [], []
    total = jnp.int32(0)
    for s in range(slides_n):
        total = total + slide_units[s] * PAD
        ends.append(total)
        lims.append(total - shortfall[s])

    def label_of(pos):
        lab = jnp.zeros(pos.shape, jnp.int32)
        for s in range(slides_n - 1):
            lab = lab + jnp.where(pos >= ends[s], 1, 0)
        return lab

    def code_of(pos):
        code = label_of(pos)
        for s in range(slides_n):
            code = jnp.where((pos >= lims[s]) & (pos < ends[s]), -1, code)
        return code

    seg_first = r * 1024

    vec[...] = jnp.zeros(vec.shape, F32)
    for s in range(4):
        for h in range(4):
            wop[s, 64 * h + 48 : 64 * h + 64, :] = jnp.zeros((16, 768), BF16)
    sel_f, sel_j = iota((768, 256), 0), iota((768, 256), 1)
    head_sel = onehot((sel_f == 192 * c + 48 * (sel_j >> 6) + (sel_j & 63)) & ((sel_j & 63) < 48))
    for i, d in enumerate(in_qkv):
        d.wait()
        wqkv[:, 256 * i : 256 * i + 256] = nn(wup[:, 768 * i : 768 * i + 768], head_sel).astype(BF16)
    in_up.start()
    bqkv[...] = jnp.zeros(bqkv.shape, F32)
    biases = moved(par[0:8, :], head_sel)
    bqkv[0:1, 0:256] = biases[2:3]
    bqkv[0:1, 512:768] = biases[3:4]

    def qkv_block(b):
        x = tok[b].astype(F32)
        unit, _ = normalise(x)
        low = (unit * par[0:1, :] + par[1:2, :]).astype(BF16)
        a1[b] = low
        y = (nn(low, wqkv[...]) + bqkv[0:1, :]).astype(BF16).astype(F32)
        at = pl.ds(pl.multiple_of(256 * b, 256), 256)
        for i in range(6):
            qf[i, at, :] = y[:, 128 * i : 128 * i + 128]
        lane = iota((256, 128), 1) & 63
        key_code = code_of(seg_first + 256 * b + iota((256, 128), 0))
        key_mark = jnp.where(key_code == lane - 48, 0.0, NEG)
        marked = (lane >= 48) & (lane < 48 + slides_n)
        for p in range(2):
            qrow[p, at, :] = y[:, 128 * p : 128 * p + 128].astype(BF16)
            kaug[p, at, :] = jnp.where(marked, key_mark, y[:, 256 + 128 * p : 384 + 128 * p]).astype(BF16)
            vaug[p, at, :] = jnp.where(
                (lane == 48) | (lane == 49), 1.0, y[:, 512 + 128 * p : 640 + 128 * p]
            ).astype(BF16)
        qt, ktv, vt = y[:, :256].T, y[:, 256:512].T, y[:, 512:].T
        row = iota((128, 256), 0)
        query_label = label_of(seg_first + 256 * b + iota((128, 256), 1))
        mark = jnp.where(query_label == (row & 63) - 48, 1.0, 0.0)
        for h in range(4):
            p, half = h // 2, h % 2
            own = (row >> 6) == half
            full = jnp.where((row & 63) < 48, qt[128 * p : 128 * p + 128], mark)
            qtm[h, b] = jnp.where(own, full, 0.0).astype(BF16)
            hq, hk, hv = (m[64 * h : 64 * h + 64] for m in (qt, ktv, vt))
            kt[h, b] = hk.astype(BF16)
            vta[h, b] = jnp.where(iota((64, 256), 0) == 48, 1.0, hv).astype(BF16)
            sdr[h, b] = jnp.broadcast_to(colsum(hq * hk) * SCALE2, (8, 256))

    qkv_block(c)
    g_tok.near.wait_recv()
    qkv_block(sib)
    g_tok.forward()
    qkv_block(across)

    in_up.wait()
    for n in range(3):
        lo = (4 * share * ((256 * n) // share)) // 128 * 128
        hi = -(-(4 * share * ((256 * n + 255) // share + 1)) // 128) * 128
        o = 256 * n + iota((hi - lo, 256), 1)
        group = jnp.zeros_like(o)
        for t in range(1, rows_n):
            group = group + jnp.where(o >= share * t, 1, 0)
        unit_sel = onehot(lo + iota((hi - lo, 256), 0) == 3 * share * group + share * c + o)
        for m in range(3):
            wupq[256 * m : 256 * m + 256, 256 * n : 256 * n + 256] = nn(
                wup[256 * m : 256 * m + 256, lo:hi], unit_sel
            ).astype(BF16)
        pieces = [par[8 + t : 9 + t, :] for t in range(4)]
        line = jnp.concatenate(pieces, axis=1)[:, lo:hi]
        bupq[0:8, 256 * n : 256 * n + 256] = moved(jnp.broadcast_to(line, (8, hi - lo)), unit_sel)

    g_tok.hand.wait_recv()
    qkv_block(diag)
    g_cot.forward()

    half_lane = iota((64, 128), 1) < 64

    def picked(i, h):
        return qf[i, pl.ds(LOCAL_HEADS * c + h, 64, stride=STRIDE), :]

    for i in range(4):
        p = i % 2
        kvs[r, :, 128 * i : 128 * i + 128] = jnp.where(
            half_lane, picked(2 + i, 2 * p), picked(2 + i, 2 * p + 1)
        ).astype(BF16)
    for h in range(4):
        own = (iota((64, 128), 1) >> 6) == h % 2
        qsel[h] = jnp.where(own, picked(h // 2, h), 0.0).astype(BF16)

    def sparse_copy(j):
        return remote(kvs.at[r], kvs.at[r], sps.at[j - 1], spr.at[j - 1], ((r + j) % rows_n, c))

    def each_row(fn):
        def step(j, carry):
            fn(j)
            return carry

        lax.fori_loop(1, rows_n, step, 0)

    each_row(lambda j: sparse_copy(j).start())

    eye = iota((256, 256), 0) == iota((256, 256), 1)

    def weights_out(i):
        return pltpu.make_async_copy(pbuf.at[i % 2], p_h.at[i], psem.at[i % 2])

    def forward_tile(i):
        h, ib = i // 4, i % 4
        p, half = h // 2, h % 2
        slot = i % 2
        rhs = qtm[h, ib]
        top = jnp.full((8, 256), NEG * 10, F32)
        for jb in range(4):
            s = nn(kaug[p, 256 * jb : 256 * jb + 256, :], rhs) * SCALE2
            sref[256 * jb : 256 * jb + 256, :] = s
            top = jnp.maximum(top, jnp.max(s.reshape(32, 8, 256), axis=0))
        own = sdr[h, ib]
        top = jnp.max(jnp.maximum(top, own), axis=0, keepdims=True)
        at = pl.ds(pl.multiple_of(256 * ib, 256), 256)
        sref[at, :] = jnp.where(eye, own[0:1], sref[at, :])

        @pl.when(i >= 2)
        def _():
            weights_out(i).wait()

        for jb in range(4):
            pbuf[slot, 256 * jb : 256 * jb + 256, :] = jnp.exp2(
                sref[256 * jb : 256 * jb + 256, :] - top
            ).astype(BF16)
        weights_out(i).start()
        values = jnp.concatenate([vta[h, jb] for jb in range(4)], axis=1)
        o = nn(values, pbuf[slot])
        z = o[48:49]
        inverse = 1.0 / z
        line = iota((64, 256), 0)
        o = o * inverse
        o = jnp.where(line == 48, inverse, jnp.where(line == 49, top, jnp.where(line == 50, z, o)))
        dqt[half, ib] = o

    def branch_b(h):
        p, half = h // 2, h % 2
        lane = iota((64, 128), 1)
        k2 = kvs[:, :, 128 * p : 128 * p + 128].reshape(key_count, 128)
        v2 = kvs[:, :, 256 + 128 * p : 384 + 128 * p].reshape(key_count, 128)
        s = nt(qsel[h], k2) * SCALE2
        first = LOCAL_HEADS * c + h
        qpos = seg_first + STRIDE * iota((64, 128), 0)[:, 0:1] + first
        kpos = STRIDE * iota((8, key_count), 1)[0:1] + first
        s = jnp.where((label_of(qpos) == code_of(kpos)) | (qpos == kpos), s, NEG)
        top_b = jnp.max(s, axis=1, keepdims=True)
        e = jnp.exp2(s - top_b)
        z_b = jnp.sum(e, axis=1, keepdims=True)
        o_b = nn(e.astype(BF16), v2)
        at = pl.ds(first, 64, stride=STRIDE)
        old = oa[p, at, :]
        top_a = old[:, 64 * half + 49 : 64 * half + 50]
        z_a = old[:, 64 * half + 50 : 64 * half + 51]
        top = jnp.maximum(top_a, top_b)
        in_a, in_b = jnp.exp2(top_a - top), jnp.exp2(top_b - top)
        inverse = 1.0 / (in_a * z_a + in_b * z_b)
        o = (in_a * z_a * old + in_b * o_b) * inverse
        own = (lane >> 6) == half
        new = jnp.where(own & ((lane & 63) < 48), o, jnp.where(lane == 64 * half + 48, in_a * inverse, old))
        oa[p, at, :] = new
        wb[h] = (e * (in_b * inverse)).astype(wb.dtype)

    lane256 = iota((256, 128), 1)
    for p in range(2):
        def fwd(t, carry, p=p):
            forward_tile(8 * p + t)
            return carry

        lax.fori_loop(0, 8, fwd, 0)
        for ib in range(4):
            oa[p, 256 * ib : 256 * ib + 256, :] = jnp.concatenate([dqt[0, ib], dqt[1, ib]], axis=0).T
        if p == 0:
            each_row(lambda j: sparse_copy(j).wait_recv())
        branch_b(2 * p)
        branch_b(2 * p + 1)
        for ib in range(4):
            att[c, p, ib] = jnp.where(
                (lane256 & 63) < 48, oa[p, 256 * ib : 256 * ib + 256, :], 0.0
            ).astype(BF16)
        g_att[p].start()
    weights_out(14).wait()
    weights_out(15).wait()
    g_cot.near.wait_recv()
    g_cot.hand.wait_recv()
    vec[5:6, :] = colsum(gb[...].reshape(1024, 768).astype(F32))
    for d in in_wo:
        d.wait()
    for p in range(2):
        g_att[p].forward()
    for p in range(2):
        g_att[p].near.wait_recv()
        g_att[p].hand.wait_recv()

    def project(b):
        out = tok[b].astype(F32) + par[4:5, :]
        for s in range(4):
            out = out + nn(jnp.concatenate([att[s, 0, b], att[s, 1, b]], axis=1), wop[s])
        return out

    def second_norm(b, values):
        unit, inverse = normalise(values)
        a2[b] = (unit * par[5:6, :] + par[6:7, :]).astype(BF16)
        return unit, inverse

    y1[...] = project(c)
    second_norm(c, y1[...])

    in_dn.wait()
    acc[...] = y1[...] + par[7:8, :]
    da2[...] = jnp.zeros(da2.shape, F32)

    def mlp(i, carry):
        low = a2[c]
        g = gb[c]
        at = pl.ds(pl.multiple_of(768 * i, 768), 768)
        u = nn(low, wup[:, at]) + par[pl.ds(8 + i, 1), :]
        hidden, slope = gelu_parts(u)
        acc[...] += nn(hidden.astype(BF16), wdn[at, :])
        du = (nt(g, wdn[at, :]) * slope).astype(BF16)
        da2[...] += nt(du, wup[:, at])
        return carry

    lax.fori_loop(0, 4, mlp, 0)
    wqkv[0:256, :] = acc[...].astype(BF16)
    out_copy = local(wqkv.at[pl.ds(0, 256), :], out_h, 0)
    out_copy.start()
    unit, inverse = normalise(y1[...])
    vec[3:4, :] = colsum(da2[...] * unit)
    vec[4:5, :] = colsum(da2[...])
    dy1 = gb[c].astype(F32) + norm_back(da2[...], unit, inverse, par[5:6, :])
    y1[...] = dy1
    drb[c] = dy1.astype(BF16)
    g_dr.start()

    for j in range(1, 4):
        b = (c + j) % 4
        second_norm(b, project(b))
    in_dq.wait()

    def quarter(b, carry):
        u = nn(a2[b], wupq[...]) + bupq[0:1, :]
        hidden, slope = gelu_parts(u)
        at = pl.ds(pl.multiple_of(256 * b, 256), 256)
        wdn[at, :] = hidden.astype(BF16)
        du = (nt(gb[b], wdq[...]) * slope).astype(BF16)
        wdn[pl.ds(pl.multiple_of(1024 + 256 * b, 256), 256), :] = du
        vec[6:7, :] += colsum(du.astype(F32))
        return carry

    lax.fori_loop(0, 4, quarter, 0)

    def put(n, block, first):
        buf = slabs[n]
        width = block.shape[1]
        at = first
        while at < first + block.shape[0]:
            which, off = at // share, at % share
            size = min(share - off, first + block.shape[0] - at)
            buf[which % 2, which // 2, off : off + size, 0:width] = block[at - first : at - first + size].astype(BF16)
            at += size

    def phase_one(n):
        return remote(slabs[n].at[1 - rbit], recv_a[n], u1s.at[n], u1r.at[n], (2 * ra + 1 - rbit, c))

    def phase_two(n, j):
        to = (ra + j) % row_a
        return remote(slabs[n].at[rbit, to], recv_b[n].at[j - 1], u2s.at[n, j - 1], u2r.at[n, j - 1], (2 * to + rbit, c))

    def start_two(n):
        phase_one(n).wait_recv()

        def add(i, carry):
            slabs[n][rbit, i] = (slabs[n][rbit, i].astype(F32) + recv_a[n][i].astype(F32)).astype(BF16)
            return carry

        lax.fori_loop(0, row_a, add, 0)

        def send(j, carry):
            phase_two(n, j).start()
            return carry

        lax.fori_loop(1, row_a, send, 0)

    def slab_sent(n):
        phase_one(n).wait_send()

        def sent(j, carry):
            phase_two(n, j).wait_send()
            return carry

        lax.fori_loop(1, row_a, sent, 0)

    def col_copy(n, j):
        at = pl.ds(OFFSETS[n], UNITS[n])
        return remote(gath.at[c, :, at], gath.at[c, :, at], ucs.at[n, j - 1], ucr.at[n, j - 1], (r, (c + j) % COLS))

    def finish(n):
        def wait(j, carry):
            phase_two(n, j).wait_recv()
            return carry

        lax.fori_loop(1, row_a, wait, 0)
        gath[c, :, OFFSETS[n] : OFFSETS[n] + UNITS[n]] = (
            lax.fori_loop(
                0, row_a - 1, lambda j, t: t + recv_b[n][j].astype(F32), slabs[n][rbit, ra].astype(F32)
            )
        ).astype(BF16)
        for j in range(1, COLS):
            col_copy(n, j).start()

    for m in range(2):
        put(0, tn(wdn[0:1024, 384 * m : 384 * m + 384], gb[...].reshape(1024, 768)), 384 * m)
    phase_one(0).start()
    g_dr.forward()
    for m in range(2):
        lanes = jnp.concatenate([a2[b, :, 384 * m : 384 * m + 384] for b in range(4)], axis=0)
        put(1, tn(lanes, wdn[1024:2048, :]), 384 * m)
    phase_one(1).start()

    g_dr.near.wait_recv()
    g_dr.hand.wait_recv()
    vec[2:3, :] = colsum(drb[...].reshape(1024, 768).astype(F32))
    bones = onehot((iota((256, 256), 0) >> 6) == (iota((256, 256), 1) >> 6))

    def out_grad(b, carry):
        lane = iota((256, 256), 1) & 63
        at = pl.ds(pl.multiple_of(256 * b, 256), 256)
        d_att = nt(drb[b], wop[c]).astype(BF16).astype(F32)
        attended = jnp.concatenate([att[c, 0, b], att[c, 1, b]], axis=1).astype(F32)
        rowsum = moved(d_att * attended, bones, 2)
        factor = moved(
            jnp.where(lane == 48, jnp.concatenate([oa[0, at, :], oa[1, at, :]], axis=1), 0.0), bones
        )
        minus = -rowsum * factor
        high = minus.astype(BF16).astype(F32)
        marked = jnp.where(lane == 48, high, jnp.where(lane == 49, minus - high, d_att * factor))
        flipped = marked.T
        line = iota((128, 256), 0)
        for p in range(2):
            kaug[p, at, :] = marked[:, 128 * p : 128 * p + 128].astype(BF16)
            qf[p, at, :] = d_att[:, 128 * p : 128 * p + 128]
            qf[2 + p, at, :] = rowsum[:, 128 * p : 128 * p + 128]
        for h in range(4):
            p = h // 2
            qtm[h, b] = jnp.where(
                (line >> 6) == h % 2, flipped[128 * p : 128 * p + 128], 0.0
            ).astype(BF16)
        return carry

    lax.fori_loop(0, 4, out_grad, 0)

    own_cols = onehot(
        (iota((256, 768), 1) == 192 * c + iota((256, 768), 0)) & (iota((256, 768), 0) < 192)
    )
    dr_own = jnp.concatenate([nt(own_cols, drb[b]).astype(BF16) for b in range(4)], axis=1)
    for s in range(4):
        both = jnp.concatenate(
            [att[s, 0].reshape(1024, 128), att[s, 1].reshape(1024, 128)], axis=1
        )
        block = nn(dr_own, both).T
        for h in range(4):
            put(2, block[64 * h : 64 * h + 48], 192 * s + 48 * h)
    phase_one(2).start()

    step_rows = min(rows_n, 8)
    step_keys = 64 * step_rows

    def dilated_block(t):
        tall, wide = pl.multiple_of(64 * (t // 6), 64), pl.multiple_of(512 * (t % 6), 512)
        return wup.at[pl.ds(tall, 64), pl.ds(wide, 512)]

    for p in range(2):
        sides = []
        for half in range(2):
            h = 2 * p + half
            own = (iota((64, 128), 1) >> 6) == half
            d_sel = jnp.where(own, picked(p, h), 0.0).astype(BF16)
            sides.append((h, d_sel, picked(2 + p, h)[:, 64 * half : 64 * half + 1]))
            dqb[h] = jnp.zeros((64, 128), F32)

        def some_keys(n, carry, p=p, sides=sides):
            some = pl.ds(pl.multiple_of(step_rows * n, step_rows), step_rows)
            k2 = kvs[some, :, 128 * p : 128 * p + 128].reshape(step_keys, 128)
            v2 = kvs[some, :, 256 + 128 * p : 384 + 128 * p].reshape(step_keys, 128)
            dk, dv = 0.0, 0.0
            for h, d_sel, rs in sides:
                own = (iota((64, 128), 1) >> 6) == h % 2
                w = wb[h, :, pl.ds(pl.multiple_of(step_keys * n, step_keys), step_keys)]
                ds = (w.astype(F32) * (nt(d_sel, v2) - rs)).astype(BF16)
                dqb[h] += jnp.where(own, nn(ds, k2), 0.0)
                dk = dk + tn(ds, qsel[h])
                dv = dv + tn(w, d_sel)
            for t in range(step_rows):
                block = dilated_block(step_rows * n + t)
                block[:, 128 * p : 128 * p + 128] = dk[64 * t : 64 * t + 64].astype(BF16)
                block[:, 256 + 128 * p : 384 + 128 * p] = dv[64 * t : 64 * t + 64].astype(BF16)
            return carry

        lax.fori_loop(0, rows_n // step_rows, some_keys, 0)

    def dilated_copy(j):
        to = (r + j) % rows_n
        return remote(dilated_block(to), dkvr.at[j - 1], bss.at[j - 1], bsr.at[j - 1], (to, c))

    each_row(lambda j: dilated_copy(j).start())

    qf[...] = jnp.zeros(qf.shape, F32)

    def weights_in(i):
        return pltpu.make_async_copy(p_h.at[i], pbuf.at[i % 2], psem.at[i % 2])

    def backward_tile(i):
        h, ib = i // 4, i % 4
        p, half = h // 2, h % 2
        slot = i % 2
        weights_in(i).wait()

        @pl.when(i + 1 < 16)
        def _():
            weights_in(i + 1).start()

        rhs = qtm[h, ib]
        for jb in range(4):
            at = slice(256 * jb, 256 * jb + 256)
            dsb[at, :] = (pbuf[slot, at, :].astype(F32) * nn(vaug[p, at, :], rhs)).astype(BF16)
        keys = jnp.concatenate([kt[h, jb] for jb in range(4)], axis=1)
        dqt[h, ib] = nn(keys, dsb[...])
        at = pl.ds(pl.multiple_of(256 * ib, 256), 256)
        own = (iota((256, 128), 1) >> 6) == half
        d_rows, q_rows = kaug[p, at, :], qrow[p, at, :]
        for jb in range(4):
            js = slice(256 * jb, 256 * jb + 256)
            qf[2 + p, js, :] += jnp.where(own, nn(dsb[js, :], q_rows), 0.0)
            qf[4 + p, js, :] += jnp.where(own, nn(pbuf[slot, js, :], d_rows), 0.0)

    weights_in(0).start()
    for part in range(4):
        def bwd(t, carry, part=part):
            backward_tile(4 * part + t)
            return carry

        lax.fori_loop(0, 4, bwd, 0)
        if part == 0:
            start_two(0)
        if part == 1:
            start_two(1)
        if part == 2:
            start_two(2)

    each_row(lambda j: dilated_copy(j).wait_recv())
    spread = lax.fori_loop(
        0, rows_n - 1, lambda j, t: t + dkvr[j].astype(F32), dilated_block(r)[...].astype(F32)
    )
    each_row(lambda j: dilated_copy(j).wait_send())
    back_qkv = [local(h, wup.at[:, pl.ds(768 * i, 768)], 2 + i) for i, h in enumerate((wq_h, wk_h, wv_h))]
    for d in back_qkv:
        d.start()
    for h in range(4):
        p = h // 2
        own = (iota((64, 128), 1) >> 6) == h % 2
        at = pl.ds(LOCAL_HEADS * c + h, 64, stride=STRIDE)
        qf[p, at, :] += dqb[h]
        qf[2 + p, at, :] += jnp.where(own, spread[:, 128 * p : 128 * p + 128], 0.0)
        qf[4 + p, at, :] += jnp.where(own, spread[:, 256 + 128 * p : 384 + 128 * p], 0.0)

    def turned(i, b):
        at = pl.ds(pl.multiple_of(256 * b, 256), 256)
        return jnp.concatenate([qf[2 * i, at, :], qf[2 * i + 1, at, :]], axis=1).T

    def compact(b, carry):
        dq = (jnp.concatenate([dqt[h, b] for h in range(4)], axis=0) + turned(0, b)) * SCALE
        for i, m in enumerate((dq, turned(1, b) * SCALE, turned(2, b))):
            for h in range(4):
                a2[b, 48 * h : 48 * h + 48, 256 * i : 256 * i + 256] = m[64 * h : 64 * h + 48].astype(BF16)
        return carry

    lax.fori_loop(0, 4, compact, 0)

    def exchange(j):
        to = (c + j) % COLS
        at = pl.ds(pl.multiple_of(192 * c, 64), 192)
        return remote(a2.at[to, pl.ds(0, 192), :], dqr.at[at, :], ats.at[j - 1], atr.at[j - 1], (r, to))

    for j in range(1, COLS):
        exchange(j).start()
    dqr[pl.ds(pl.multiple_of(192 * c, 64), 192), :] = a2[c, 0:192, :]
    finish(0)
    finish(1)

    rows576 = [
        jnp.concatenate(
            [a2[b, 0:192, 256 * i : 256 * i + 256] for i in range(3)] + [jnp.zeros((64, 256), BF16)], axis=0
        )
        for b in range(4)
    ]
    lhs = jnp.concatenate(rows576, axis=1)
    slab_sent(0)
    for m in range(2):
        lanes = jnp.concatenate([a1[b, :, 384 * m : 384 * m + 384] for b in range(4)], axis=0)
        put(3, nn(lhs, lanes).T, 384 * m)
    phase_one(3).start()
    ones = jnp.ones((16, 1024), BF16)
    vec[7:8, 0:640] = nt(ones, lhs)[0:1]
    finish(2)

    for d in back_qkv:
        d.wait()
    for j in range(1, COLS):
        exchange(j).wait_recv()
    da1 = nn(wup[:, 0:768], dqr[:, 0:256])
    for i in range(1, 3):
        da1 = da1 + nn(wup[:, 768 * i : 768 * i + 768], dqr[:, 256 * i : 256 * i + 256])
    da1 = da1.T
    unit, inverse = normalise(tok[c].astype(F32))
    vec[0:1, :] = colsum(da1 * unit)
    vec[1:2, :] = colsum(da1)
    vec_pair = remote(vec, vpair, vss.at[0], vsr.at[0], (2 * ra + 1 - rbit, c))
    vec_pair.start()
    start_two(3)
    da2[...] = y1[...] + norm_back(da1, unit, inverse, par[0:1, :])
    gt_copy = local(da2, gt_h, 1)
    gt_copy.start()

    vec_pair.wait_recv()
    vrow[ra] = vec[...] + vpair[...]

    def vec_copy(j):
        to = (ra + j) % row_a
        return remote(vrow.at[ra], vrow.at[ra], vss.at[j], vsr.at[j], (2 * to + rbit, c))

    def each_pair(fn):
        def step(j, carry):
            fn(j)
            return carry

        lax.fori_loop(1, row_a, step, 0)

    each_pair(lambda j: vec_copy(j).start())
    finish(3)
    each_pair(lambda j: vec_copy(j).wait_recv())
    vcol[c] = lax.fori_loop(0, row_a, lambda j, t: t + vrow[j], jnp.zeros((16, 768), F32))

    def vec_col(j):
        return remote(vcol.at[c], vcol.at[c], vcs.at[j - 1], vcr.at[j - 1], (r, (c + j) % COLS))

    for j in range(1, COLS):
        vec_col(j).start()
    for j in range(1, COLS):
        vec_col(j).wait_recv()
        for n in range(4):
            col_copy(n, j).wait_recv()
    out_gath = local(gath, gath_h, 2)
    out_vec = local(vcol, vec_h, 3)
    out_gath.start()
    out_vec.start()

    for g in (g_tok, g_cot, *g_att, g_dr):
        g.drain()
    each_row(lambda j: sparse_copy(j).wait_send())
    vec_pair.wait_send()
    each_pair(lambda j: vec_copy(j).wait_send())
    for n in range(4):
        if n:
            slab_sent(n)
        for j in range(1, COLS):
            col_copy(n, j).wait_send()
    for j in range(1, COLS):
        exchange(j).wait_send()
        vec_col(j).wait_send()
    out_copy.wait()
    gt_copy.wait()
    out_gath.wait()
    out_vec.wait()


def finale(rows_n, gath, vec, out_in, gt_in, out, gt, g1, b1, gq, bq, gk, gv, bv, go, bo, g2, b2, gu, bu, gd, bd):
    share = 768 // rows_n
    r = lax.axis_index("row")
    out[...] = out_in[...]
    gt[...] = gt_in[...]
    part = [gath[s].astype(F32)[:share] for s in range(COLS)]

    def across(off, width):
        return jnp.concatenate([part[s][:, off : off + width] for s in range(COLS)], axis=1)

    gq[...] = across(1792, 192)
    gk[...] = across(1792 + 192, 192)
    gv[...] = across(1792 + 384, 192)
    go[...] = across(1536, 192)
    gu[...] = jnp.concatenate(
        [part[s][:, 768 + share * t : 768 + share * t + share] for t in range(rows_n) for s in range(COLS)], axis=1
    )
    for s in range(COLS):
        gd[share * s : share * s + share, :] = part[s][:, 0:768]
    summed = vec[0] + vec[1] + vec[2] + vec[3]
    wide = max(128, -(-share // 128) * 128)
    f, j = iota((768, wide), 0), iota((768, wide), 1)
    pick = onehot((f == share * r + j) & (j < share))
    mine = vec[0]
    total = moved(jnp.concatenate([summed[0:8], mine[0:8]], axis=0), pick)
    hidden = [moved(vec[s][0:8], pick) for s in range(COLS)]
    qv = [None, None]
    for n, off in enumerate((0, 384)):
        for s in range(COLS):
            place = onehot((f + 192 * s - off == share * r + j) & (j < share) & (f >= off) & (f < off + 192))
            term = moved(vec[s][0:8], place)
            qv[n] = term if qv[n] is None else qv[n] + term
    g1[...] = total[0, :share]
    b1[...] = total[1, :share]
    bo[...] = total[8 + 2, :share]
    g2[...] = total[3, :share]
    b2[...] = total[4, :share]
    bd[...] = total[8 + 5, :share]
    bq[...] = qv[0][7, :share]
    bv[...] = qv[1][7, :share]
    bu[...] = jnp.concatenate([hidden[s][6:7, :share] for s in range(COLS)], axis=1)[0]


def body(rows_n, tokens, norm1_gain, norm1_bias, w_query, b_query, w_key, w_value, b_value, w_out, b_out,
         norm2_gain, norm2_bias, w_up, b_up, w_down, b_down, slide_padded_units, padding_shortfall, cotangent):
    row_a, share = rows_n // 2, 768 // rows_n
    padded = -(-share // 16) * 16
    c = lax.axis_index("col")
    par = jnp.concatenate(
        [
            jnp.stack([norm1_gain, norm1_bias, b_query, b_value, b_out, norm2_gain, norm2_bias, b_down]),
            b_up.reshape(4, 768),
            jnp.zeros((4, 768), F32),
        ]
    )
    down_q = lax.dynamic_index_in_dim(w_down.reshape(rows_n, COLS, share, 768), c, 1, False).reshape(768, 768)
    vmem = pltpu.VMEM
    dma = pltpu.SemaphoreType.DMA
    between = max(row_a - 1, 1)
    scratch = [
        vmem((768, 3072), BF16), vmem((3072, 768), BF16), vmem((768, 768), BF16), vmem((768, 768), BF16),
        vmem((768, 768), BF16), vmem((4, 256, 768), BF16),
        *[vmem((4, 256, 768), BF16) for _ in range(5)],
        vmem((6, 1040, 128), F32), vmem((2, 1024, 128), BF16), vmem((2, 1024, 128), BF16),
        vmem((2, 1024, 128), BF16), vmem((4, 4, 128, 256), BF16), vmem((4, 4, 64, 256), BF16),
        vmem((4, 4, 64, 256), BF16), vmem((4, 4, 8, 256), F32),
        vmem((2, 1024, 256), BF16), vmem((1024, 256), F32), vmem((1024, 256), BF16),
        vmem((2, 1040, 128), F32), vmem((4, 2, 4, 256, 128), BF16),
        vmem((256, 768), F32), vmem((256, 768), F32), vmem((256, 768), F32),
        vmem((4, 4, 64, 256), F32), vmem((768, 768), BF16),
        *[vmem((2, row_a, padded, w), BF16) for w in UNITS[:3]],
        *[vmem((row_a, padded, w), BF16) for w in UNITS],
        *[vmem((between, padded, w), BF16) for w in UNITS],
        vmem((4, padded, WIDTH), BF16),
        vmem((rows_n, 64, 512), BF16), vmem((4, 64, 128), BF16), vmem((4, 64, rows_n * 64), BF16),
        vmem((4, 64, 128), F32), vmem((rows_n - 1, 64, 512), BF16),
        vmem((16, 768), F32), vmem((16, 768), F32), vmem((row_a, 16, 768), F32), vmem((4, 16, 768), F32), vmem((8, 768), F32),
        vmem((8, 768), F32),
        dma((24,)), dma((5, 3)), dma((5, 3)), dma((rows_n - 1,)), dma((rows_n - 1,)), dma((rows_n - 1,)),
        dma((rows_n - 1,)), dma((4,)), dma((4,)), dma((4, between)), dma((4, between)), dma((4, 3)), dma((4, 3)),
        dma((3,)), dma((3,)), dma((row_a,)), dma((row_a,)), dma((3,)), dma((3,)), dma((2,)),
    ]
    hbm = pl.BlockSpec(memory_space=pl.ANY)
    smem = pl.BlockSpec(memory_space=pltpu.SMEM)
    whole = pl.BlockSpec(memory_space=pltpu.VMEM)
    sds = jax.ShapeDtypeStruct
    out, gt, gath, vec, _ = pl.pallas_call(
        functools.partial(layer, rows_n, slide_padded_units.shape[0], None),
        out_shape=(
            sds((256, 768), BF16), sds((256, 768), F32), sds((4, padded, WIDTH), BF16), sds((4, 16, 768), F32),
            sds((16, 1024, 256), BF16),
        ),
        in_specs=[smem, smem, whole] + [hbm] * 9,
        out_specs=(hbm,) * 5,
        scratch_shapes=scratch,
        compiler_params=pltpu.CompilerParams(
            collective_id=0, has_side_effects=True, vmem_limit_bytes=(992 if rows_n <= 8 else 1021) * 64 * 1024
        ),
        name="layer",
    )(slide_padded_units, padding_shortfall, par, tokens, cotangent, w_query, w_key, w_value, w_out, w_up, w_down,
      down_q)
    vec1 = sds((share,), F32)
    mat = sds((share, 768), F32)
    return pl.pallas_call(
        functools.partial(finale, rows_n),
        out_shape=(
            sds((256, 768), BF16), sds((256, 768), F32), vec1, vec1, mat, vec1, mat, mat, vec1, mat, vec1, vec1, vec1,
            sds((share, 3072), F32), sds((4 * share,), F32), sds((4 * share, 768), F32), vec1,
        ),
        in_specs=[whole] * 4,
        out_specs=(whole,) * 17,
        compiler_params=pltpu.CompilerParams(vmem_limit_bytes=48 * 1024 * 1024),
        name="finale",
    )(gath, vec, out, gt)


def solution(mesh):
    tiles = P(("row", "col"), None)
    one, two = P("row"), P("row", None)
    return jax.shard_map(
        functools.partial(body, mesh.shape["row"]),
        mesh=mesh,
        in_specs=(tiles,) + (P(),) * 17 + (tiles,),
        out_specs=(tiles, tiles, one, one, two, one, two, two, one, two, one, one, one, two, one, two, one),
        check_vma=False,
    )
```

time: 1240 us -> 173 us (0.14); the launches traced: 1220 us -> 170 us
  waiting for transfers between devices: 684 us -> 0 us
  matrix products: 159 us -> 0 us
  Pallas kernels: 0 us -> 155 us
  blocking collectives: 126 us -> 0 us
  local copies, waits for them, and re-layouts: 134 us -> 14.4 us
  other arithmetic: 98.8 us -> 0 us
  between operations: 18.6 us -> 0.86 us
    reduce_scatter x8 -> x0, waiting for transfers between devices: 625 us -> none  [the longest x1 165 us: body(): lax.psum_scatter(g_w_up, 'row', scatter_dimension=0, tiled=True)]
    dot_general x70 -> x0, matrix products: 159 us -> none  [the longest x18 57.1 us: product(): return jnp.dot(left, right, preferred_element_type=jnp.float32)]
    pallas_call x0 -> x2, Pallas kernels: none -> 155 us  [the longest x1 152 us: body(): pl.pallas_call(functools.partial(layer, rows_n, slide_padded_units.shape[...]
    all_gather x2 -> x0, blocking collectives: 84.4 us -> none  [the longest x1 45.3 us: body(): lax.all_gather(v_sel, ('row', 'col'), axis=0, tiled=True)]
    unnamed x15 -> x0, waiting for transfers between devices: 59.3 us -> none
    convert_element_type x28 -> x0, other arithmetic: 48.1 us -> none  [the longest x1 15 us: body(): ds_a = (weights_a * (dw_a - row_full[:, :, None])).astype(jnp.bfloat16)]
    slice x33 -> x0, local copies, waits for them, and re-layouts: 40.8 us -> none  [the longest x5 10.1 us: body(): seg_values[:, column_lower:column_upper]]
    reshape x38 -> x1, local copies, waits for them, and re-layouts: 36.9 us -> 0.72 us  [body(): b_up.reshape(4, 768)]
  transfers between devices with their start and end apart: 13 -> 0, of which waited for: 9 -> 0; matrix products, arithmetic and copies ran while one was open for 22% -> 0% of each run, Pallas kernels for 0% -> 0%
where the time goes in v1:
time: 173 us; the launch traced here: 170 us
  Pallas kernels  155 us (90%)
  local copies, waits for them, and re-layouts  14.4 us (8%)
    pallas_call x1, Pallas kernels, body(): pl.pallas_call(functools.partial(layer, rows_n, slide_padded_units.shape[...  152 us
    another operation x8, local copies, waits for them, and re-layouts, body(): jnp.stack([norm1_gain, norm1_bias, b_query, b_value, b_out, norm2_gain, n...  5.51 us
    unnamed x8, local copies, waits for them, and re-layouts  4.56 us

profile of v1, /device:TPU:0, one launch (start us, length us, event | category | flops | bytes accessed | tf_op | source)
XLA Modules:
  0.0 170.3 jit_solution(658955392955839056)
XLA Ops:
  0.7 0.7 stack.24
  1.3 0.7 stack.25
  2.0 0.7 stack.26
  2.7 0.7 stack.27
  3.4 0.7 stack.28
  4.1 0.7 stack.29
  4.8 0.7 stack.30
  5.5 0.7 stack.31
  6.2 0.7 reshape.44
  6.9 1.3 concatenate.3.par
  8.2 2.4 %constant_dynamic-slice_fusion = bf16[8,1,96,768]{3,2,1,0:T(8,128)(2,1)} fusion(bf16[8,4,96,768]{3,2,1,0:T(8,128)(2,1)} %bitcast.4, s32[]{:T(128)S(6)} %select_n.4), kind=kLoop, calls=%fused_computation | loop fusion | bytes 2359300 | tf_op jit(solution)/shard_map/jit(dynamic_index_in_dim)/dynamic_slice | solution.py:836
  10.5 151.9 %layer.1 = (bf16[256,768]{1,0:T(8,128)(2,1)}, f32[256,768]{1,0:T(8,128)}, bf16[4,96,2432]{2,1,0:T(8,128)(2,1)}, f32[4,16,768]{2,1,0:T(8,128)}, bf16[16,1024,256]{2,1,0:T(8,128)(2,1)}) custom-call(s32[8]{0:T(128)} %slide_units.1, s32[8]{0:T(128)} %shortfall.1, f32[16,768]{1,0:T(8,128)} %concatenate.3.par, bf16[256,768]{1,0:T(8,128)(2,1)} %tok_h.1, ...), custom_call_target="tpu_custom_call" | custom-call | tf_op jit(solution)/shard_map/layer/pallas_call | solution.py:867
  162.4 0.0 copy-start
  162.4 1.5 copy-done
  163.9 0.0 copy-start.1
  163.9 1.1 copy-done.1
  165.0 0.0 copy-start.2
  165.1 1.0 copy-done.2
  166.0 0.0 copy-start.3
  166.0 0.9 copy-done.3
  167.0 3.2 %finale.1 = (bf16[256,768]{1,0:T(8,128)(2,1)}, f32[256,768]{1,0:T(8,128)}, f32[96]{0:T(128)}, f32[96]{0:T(128)}, f32[96,768]{1,0:T(8,128)}, /*index=5*/f32[96]{0...) custom-call(bf16[4,96,2432]{2,1,0:T(8,128)(2,1)S(1)} %copy-done, ...), custom_call_target="tpu_custom_call" | custom-call | tf_op jit(solution)/shard_map/finale/pallas_call | solution.py:884
  (1 shorter events, 0.0 us)
Async XLA Ops:
  162.4 1.5 copy-start
  163.9 1.1 copy-start.1
  165.0 1.0 copy-start.2
  166.0 0.9 copy-start.3

commit v2 on v1

--- a/solution.py
+++ b/solution.py
@@ -85,29 +85,31 @@
 
 
 def layer(
-    rows_n, slides_n, stop,
-    slide_units, shortfall, par, tok_h, cot_h, wq_h, wk_h, wv_h, wo_h, wup_h, wdn_h, wdq_h,
+    rows_n, slides_n, keep,
+    slide_units, shortfall, v0, v1, v2, v3, v4, v5, v6, v7, v8, tok_h, cot_h, wq_h, wk_h, wv_h, wo_h, wup_h, wdn_h, wdq_h,
     out_h, gt_h, gath_h, vec_h, p_h,
     wup, wdn, wqkv, wupq, wdq, wop,
     tok, gb, a1, a2, drb,
     qf, qrow, kaug, vaug, qtm, kt, vta, sdr,
     pbuf, sref, dsb, oa, att,
     y1, acc, da2, dqt, dqr,
-    slab0, slab1, slab2, ra0, ra1, ra2, ra3, rb0, rb1, rb2, rb3, gath,
-    kvs, qsel, wb, dqb, dkvr,
-    vec, vpair, vrow, vcol, bupq, bqkv,
-    lsem, gss, gsr, sps, spr, bss, bsr, u1s, u1r, u2s, u2r, ucs, ucr, ats, atr, vss, vsr, vcs, vcr, psem,
+    slab0, slab1, slab2, ra0, ra1, ra2, ra3, rb0, rb1, rb2, rb3, rc0, rc1, rc2, rc3, gath,
+    kvo, kvc, qsel, wb, dqb, dkvr,
+    par, vec, vin, vrow, vcol, bupq, bqkv,
+    lsem, gss, gsr, afs, afr, kos, kor, sps, spr, bss, bsr, u1s, u1r, u2s, u2r, u3s, u3r, ucs, ucr, ats, atr,
+    vss, vsr, vcs, vcr, psem,
 ):
-    row_a = rows_n // 2
+    his = rows_n // 4
     share = 768 // rows_n
     r = lax.axis_index("row")
     c = lax.axis_index("col")
     sib = c + 1 - 2 * (c % 2)
     across = (c + 2) % COLS
     diag = (sib + 2) % COLS
-    ra, rbit = r // 2, r % 2
-    recv_a, recv_b = (ra0, ra1, ra2, ra3), (rb0, rb1, rb2, rb3)
-    slabs = (slab0, slab1, slab2, slab0.at[:, :, :, pl.ds(0, UNITS[3])])
+    hi, lo, bit = r // 4, (r // 2) % 2, r % 2
+    recv_a, recv_b, recv_c = (ra0, ra1, ra2, ra3), (rb0, rb1, rb2, rb3), (rc0, rc1, rc2, rc3)
+    slabs = (slab0, slab1, slab2, wdn.at[pl.ds(0, slab0.shape[0]), pl.ds(0, UNITS[3])])
+    tall = slab0.shape[0] // rows_n
     key_count = rows_n * 64
 
     def local(src, dst, i):
@@ -118,7 +120,13 @@
     in_qkv = [local(h, wup.at[:, pl.ds(768 * i, 768)], 2 + i) for i, h in enumerate((wq_h, wk_h, wv_h))]
     in_up = local(wup_h, wup, 5)
     in_dn = local(wdn_h, wdn, 6)
-    in_dq = local(wdq_h, wdq, 7)
+    if share % 16 == 0:
+        in_dq = [
+            local(wdq_h.at[pl.ds(4 * share * t + share * c, share), :], wdq.at[pl.ds(share * t, share), :], 24 + t)
+            for t in range(rows_n)
+        ]
+    else:
+        in_dq = [local(wdq_h, wdq, 24)]
     in_wo = [
         local(wo_h.at[pl.ds(192 * s + 48 * h, 48), :], wop.at[s, pl.ds(64 * h, 48), :], 8 + 4 * s + h)
         for s in range(4)
@@ -138,7 +146,8 @@
         return carry
 
     lax.fori_loop(1, rows_n, greet, 0)
-    in_dq.start()
+    for d in in_dq:
+        d.start()
     for d in in_wo:
         d.start()
     in_dn.start()
@@ -170,13 +179,28 @@
 
     g_tok = Gather(0, lambda i: tok.at[i])
     g_cot = Gather(1, lambda i: gb.at[i])
-    g_att = [Gather(2 + p, lambda i, p=p: att.at[i, p]) for p in range(2)]
-    g_dr = Gather(4, lambda i: drb.at[i])
+    g_dr = Gather(2, lambda i: drb.at[i])
+
+    class Attended:
+        def __init__(self, p):
+            def copy(n, owner, block, dev):
+                ref = att.at[owner, p] if block is None else att.at[owner, p, block]
+                return remote(ref, ref, afs.at[p, n], afr.at[p, n], (r, dev))
+
+            self.first = [copy(0, c, None, sib), copy(1, c, across, across), copy(2, c, diag, diag)]
+            self.rest = [copy(3, c, diag, across), copy(4, c, c, across), copy(5, c, sib, across)]
+            self.hand = [copy(6, across, c, sib), copy(7, across, across, sib), copy(8, across, diag, sib)]
+
+    attended = [Attended(p) for p in range(2)]
 
     in_tok.wait()
     g_tok.start()
     in_cot.wait()
     g_cot.start()
+    for i, v in enumerate((v0, v1, v2, v3, v4, v5, v6, v7)):
+        par[i : i + 1, :] = v[...].reshape(1, 768)
+    for i in range(4):
+        par[8 + i : 9 + i, :] = v8[768 * i : 768 * i + 768].reshape(1, 768)
 
     ends, lims = [], []
     total = jnp.int32(0)
@@ -208,17 +232,40 @@
     for i, d in enumerate(in_qkv):
         d.wait()
         wqkv[:, 256 * i : 256 * i + 256] = nn(wup[:, 768 * i : 768 * i + 768], head_sel).astype(BF16)
-    in_up.start()
     bqkv[...] = jnp.zeros(bqkv.shape, F32)
     biases = moved(par[0:8, :], head_sel)
     bqkv[0:1, 0:256] = biases[2:3]
     bqkv[0:1, 512:768] = biases[3:4]
 
+    def first_norm(b):
+        unit, _ = normalise(tok[b].astype(F32))
+        a1[b] = (unit * par[0:1, :] + par[1:2, :]).astype(BF16)
+
+    first_norm(c)
+    on_head = (iota((256, 768), 0) & (STRIDE - 1)) == ((iota((256, 768), 1) * 1366) >> 16)
+
+    def dilated(values):
+        return jnp.sum(jnp.where(on_head, values.astype(BF16).astype(F32), 0.0).reshape(16, 16, 768), axis=1)
+
+    k_sel = dilated(nn(a1[c], wup[:, 768:1536]))
+    v_sel = dilated(nn(a1[c], wup[:, 1536:2304]) + par[3:4, :])
+    for s in range(COLS):
+        kvo[s] = jnp.concatenate(
+            [k_sel[:, 192 * s : 192 * s + 192], v_sel[:, 192 * s : 192 * s + 192]], axis=1
+        ).astype(BF16)
+    own16 = pl.ds(pl.multiple_of(16 * c, 16), 16)
+
+    def own_dilated(j):
+        to = (c + j) % COLS
+        return remote(kvo.at[to], kvc.at[r, own16, :], kos.at[j - 1], kor.at[j - 1], (r, to))
+
+    for j in range(1, COLS):
+        own_dilated(j).start()
+    kvc[r, own16, :] = kvo[c]
+    in_up.start()
+
     def qkv_block(b):
-        x = tok[b].astype(F32)
-        unit, _ = normalise(x)
-        low = (unit * par[0:1, :] + par[1:2, :]).astype(BF16)
-        a1[b] = low
+        low = a1[b]
         y = (nn(low, wqkv[...]) + bqkv[0:1, :]).astype(BF16).astype(F32)
         at = pl.ds(pl.multiple_of(256 * b, 256), 256)
         for i in range(6):
@@ -247,49 +294,8 @@
             vta[h, b] = jnp.where(iota((64, 256), 0) == 48, 1.0, hv).astype(BF16)
             sdr[h, b] = jnp.broadcast_to(colsum(hq * hk) * SCALE2, (8, 256))
 
-    qkv_block(c)
-    g_tok.near.wait_recv()
-    qkv_block(sib)
-    g_tok.forward()
-    qkv_block(across)
-
-    in_up.wait()
-    for n in range(3):
-        lo = (4 * share * ((256 * n) // share)) // 128 * 128
-        hi = -(-(4 * share * ((256 * n + 255) // share + 1)) // 128) * 128
-        o = 256 * n + iota((hi - lo, 256), 1)
-        group = jnp.zeros_like(o)
-        for t in range(1, rows_n):
-            group = group + jnp.where(o >= share * t, 1, 0)
-        unit_sel = onehot(lo + iota((hi - lo, 256), 0) == 3 * share * group + share * c + o)
-        for m in range(3):
-            wupq[256 * m : 256 * m + 256, 256 * n : 256 * n + 256] = nn(
-                wup[256 * m : 256 * m + 256, lo:hi], unit_sel
-            ).astype(BF16)
-        pieces = [par[8 + t : 9 + t, :] for t in range(4)]
-        line = jnp.concatenate(pieces, axis=1)[:, lo:hi]
-        bupq[0:8, 256 * n : 256 * n + 256] = moved(jnp.broadcast_to(line, (8, hi - lo)), unit_sel)
-
-    g_tok.hand.wait_recv()
-    qkv_block(diag)
-    g_cot.forward()
-
-    half_lane = iota((64, 128), 1) < 64
-
-    def picked(i, h):
-        return qf[i, pl.ds(LOCAL_HEADS * c + h, 64, stride=STRIDE), :]
-
-    for i in range(4):
-        p = i % 2
-        kvs[r, :, 128 * i : 128 * i + 128] = jnp.where(
-            half_lane, picked(2 + i, 2 * p), picked(2 + i, 2 * p + 1)
-        ).astype(BF16)
-    for h in range(4):
-        own = (iota((64, 128), 1) >> 6) == h % 2
-        qsel[h] = jnp.where(own, picked(h // 2, h), 0.0).astype(BF16)
-
     def sparse_copy(j):
-        return remote(kvs.at[r], kvs.at[r], sps.at[j - 1], spr.at[j - 1], ((r + j) % rows_n, c))
+        return remote(kvc.at[r], kvc.at[r], sps.at[j - 1], spr.at[j - 1], ((r + j) % rows_n, c))
 
     def each_row(fn):
         def step(j, carry):
@@ -298,7 +304,54 @@
 
         lax.fori_loop(1, rows_n, step, 0)
 
+    qkv_block(c)
+    g_tok.near.wait_recv()
+    first_norm(sib)
+    qkv_block(sib)
+    for j in range(1, COLS):
+        own_dilated(j).wait_recv()
     each_row(lambda j: sparse_copy(j).start())
+
+    in_up.wait()
+    for n in range(3):
+        start = (4 * share * ((256 * n) // share)) // 128 * 128
+        stop = -(-(4 * share * ((256 * n + 255) // share + 1)) // 128) * 128
+        o = 256 * n + iota((stop - start, 256), 1)
+        group = jnp.zeros_like(o)
+        for t in range(1, rows_n):
+            group = group + jnp.where(o >= share * t, 1, 0)
+        unit_sel = onehot(start + iota((stop - start, 256), 0) == 3 * share * group + share * c + o)
+        for m in range(3):
+            wupq[256 * m : 256 * m + 256, 256 * n : 256 * n + 256] = nn(
+                wup[256 * m : 256 * m + 256, start:stop], unit_sel
+            ).astype(BF16)
+        pieces = [par[8 + t : 9 + t, :] for t in range(4)]
+        line = jnp.concatenate(pieces, axis=1)[:, start:stop]
+        bupq[0:8, 256 * n : 256 * n + 256] = moved(jnp.broadcast_to(line, (8, stop - start)), unit_sel)
+
+    g_tok.forward()
+    first_norm(across)
+    qkv_block(across)
+    g_tok.hand.wait_recv()
+    first_norm(diag)
+    qkv_block(diag)
+
+    def picked(i, h):
+        return qf[i, pl.ds(LOCAL_HEADS * c + h, 64, stride=STRIDE), :]
+
+    def both_picked(i, p):
+        lane = iota((64, 128), 1)
+        return jnp.concatenate(
+            [jnp.where((lane >> 6) == half, picked(i, 2 * p + half), 0.0) for half in range(2)], axis=0
+        ).astype(BF16)
+
+    def placing(p, first, transposed=False):
+        shape = (256, 128) if transposed else (128, 256)
+        wide, narrow = iota(shape, 0 if transposed else 1), iota(shape, 1 if transposed else 0)
+        return onehot(((narrow & 63) < 48) & (wide == first + 48 * (2 * p + (narrow >> 6)) + (narrow & 63)))
+
+    for p in range(2):
+        qsel[p] = nn(both_picked(p, p), placing(p, 0)).astype(BF16)
 
     eye = iota((256, 256), 0) == iota((256, 256), 1)
 
@@ -308,7 +361,7 @@
     def forward_tile(i):
         h, ib = i // 4, i % 4
         p, half = h // 2, h % 2
-        slot = i % 2
+        slot = i if keep else i % 2
         rhs = qtm[h, ib]
         top = jnp.full((8, 256), NEG * 10, F32)
         for jb in range(4):
@@ -320,15 +373,18 @@
         at = pl.ds(pl.multiple_of(256 * ib, 256), 256)
         sref[at, :] = jnp.where(eye, own[0:1], sref[at, :])
 
-        @pl.when(i >= 2)
-        def _():
-            weights_out(i).wait()
+        if not keep:
+
+            @pl.when(i >= 2)
+            def _():
+                weights_out(i).wait()
 
         for jb in range(4):
             pbuf[slot, 256 * jb : 256 * jb + 256, :] = jnp.exp2(
                 sref[256 * jb : 256 * jb + 256, :] - top
             ).astype(BF16)
-        weights_out(i).start()
+        if not keep:
+            weights_out(i).start()
         values = jnp.concatenate([vta[h, jb] for jb in range(4)], axis=1)
         o = nn(values, pbuf[slot])
         z = o[48:49]
@@ -338,32 +394,39 @@
         o = jnp.where(line == 48, inverse, jnp.where(line == 49, top, jnp.where(line == 50, z, o)))
         dqt[half, ib] = o
 
-    def branch_b(h):
-        p, half = h // 2, h % 2
+    def branch_b(p):
         lane = iota((64, 128), 1)
-        k2 = kvs[:, :, 128 * p : 128 * p + 128].reshape(key_count, 128)
-        v2 = kvs[:, :, 256 + 128 * p : 384 + 128 * p].reshape(key_count, 128)
-        s = nt(qsel[h], k2) * SCALE2
-        first = LOCAL_HEADS * c + h
-        qpos = seg_first + STRIDE * iota((64, 128), 0)[:, 0:1] + first
-        kpos = STRIDE * iota((8, key_count), 1)[0:1] + first
-        s = jnp.where((label_of(qpos) == code_of(kpos)) | (qpos == kpos), s, NEG)
-        top_b = jnp.max(s, axis=1, keepdims=True)
-        e = jnp.exp2(s - top_b)
-        z_b = jnp.sum(e, axis=1, keepdims=True)
-        o_b = nn(e.astype(BF16), v2)
-        at = pl.ds(first, 64, stride=STRIDE)
-        old = oa[p, at, :]
-        top_a = old[:, 64 * half + 49 : 64 * half + 50]
-        z_a = old[:, 64 * half + 50 : 64 * half + 51]
-        top = jnp.maximum(top_a, top_b)
-        in_a, in_b = jnp.exp2(top_a - top), jnp.exp2(top_b - top)
-        inverse = 1.0 / (in_a * z_a + in_b * z_b)
-        o = (in_a * z_a * old + in_b * o_b) * inverse
-        own = (lane >> 6) == half
-        new = jnp.where(own & ((lane & 63) < 48), o, jnp.where(lane == 64 * half + 48, in_a * inverse, old))
-        oa[p, at, :] = new
-        wb[h] = (e * (in_b * inverse)).astype(wb.dtype)
+        s = nt(qsel[p], kvc[:, :, 0:256].reshape(key_count, 256)) * SCALE2
+        masked = []
+        for half in range(2):
+            first = LOCAL_HEADS * c + 2 * p + half
+            qpos = seg_first + STRIDE * iota((64, 128), 0)[:, 0:1] + first
+            kpos = STRIDE * iota((8, key_count), 1)[0:1] + first
+            allowed = (label_of(qpos) == code_of(kpos)) | (qpos == kpos)
+            masked.append(jnp.where(allowed, s[64 * half : 64 * half + 64], NEG))
+        s = jnp.concatenate(masked, axis=0)
+        tops = jnp.max(s, axis=1, keepdims=True)
+        e = jnp.exp2(s - tops)
+        sums = jnp.sum(e, axis=1, keepdims=True)
+        outs = moved(nn(e.astype(BF16), kvc[:, :, 128:384].reshape(key_count, 256)), placing(p, 64, True))
+        factors = []
+        for half in range(2):
+            rows = slice(64 * half, 64 * half + 64)
+            top_b, z_b, o_b = tops[rows], sums[rows], outs[rows]
+            at = pl.ds(LOCAL_HEADS * c + 2 * p + half, 64, stride=STRIDE)
+            old = oa[p, at, :]
+            top_a = old[:, 64 * half + 49 : 64 * half + 50]
+            z_a = old[:, 64 * half + 50 : 64 * half + 51]
+            top = jnp.maximum(top_a, top_b)
+            in_a, in_b = jnp.exp2(top_a - top), jnp.exp2(top_b - top)
+            inverse = 1.0 / (in_a * z_a + in_b * z_b)
+            o = (in_a * z_a * old + in_b * o_b) * inverse
+            own = (lane >> 6) == half
+            oa[p, at, :] = jnp.where(
+                own & ((lane & 63) < 48), o, jnp.where(lane == 64 * half + 48, in_a * inverse, old)
+            )
+            factors.append(in_b * inverse)
+        wb[p] = (e * jnp.concatenate(factors, axis=0)).astype(BF16)
 
     lane256 = iota((256, 128), 1)
     for p in range(2):
@@ -376,25 +439,29 @@
             oa[p, 256 * ib : 256 * ib + 256, :] = jnp.concatenate([dqt[0, ib], dqt[1, ib]], axis=0).T
         if p == 0:
             each_row(lambda j: sparse_copy(j).wait_recv())
-        branch_b(2 * p)
-        branch_b(2 * p + 1)
+        else:
+            g_cot.forward()
+        branch_b(p)
         for ib in range(4):
             att[c, p, ib] = jnp.where(
                 (lane256 & 63) < 48, oa[p, 256 * ib : 256 * ib + 256, :], 0.0
             ).astype(BF16)
-        g_att[p].start()
-    weights_out(14).wait()
-    weights_out(15).wait()
+        for d in attended[p].first:
+            d.start()
+    if not keep:
+        weights_out(14).wait()
+        weights_out(15).wait()
+    for a in attended:
+        for d in a.rest:
+            d.start()
     g_cot.near.wait_recv()
     g_cot.hand.wait_recv()
     vec[5:6, :] = colsum(gb[...].reshape(1024, 768).astype(F32))
     for d in in_wo:
         d.wait()
-    for p in range(2):
-        g_att[p].forward()
-    for p in range(2):
-        g_att[p].near.wait_recv()
-        g_att[p].hand.wait_recv()
+    for a in attended:
+        for d in a.first:
+            d.wait_recv()
 
     def project(b):
         out = tok[b].astype(F32) + par[4:5, :]
@@ -426,6 +493,11 @@
         return carry
 
     lax.fori_loop(0, 4, mlp, 0)
+    for a in attended:
+        for d in a.rest:
+            d.wait_recv()
+        for d in a.hand:
+            d.start()
     wqkv[0:256, :] = acc[...].astype(BF16)
     out_copy = local(wqkv.at[pl.ds(0, 256), :], out_h, 0)
     out_copy.start()
@@ -437,10 +509,14 @@
     drb[c] = dy1.astype(BF16)
     g_dr.start()
 
+    for a in attended:
+        for d in a.hand:
+            d.wait_recv()
     for j in range(1, 4):
         b = (c + j) % 4
         second_norm(b, project(b))
-    in_dq.wait()
+    for d in in_dq:
+        d.wait()
 
     def quarter(b, carry):
         u = nn(a2[b], wupq[...]) + bupq[0:1, :]
@@ -454,6 +530,9 @@
 
     lax.fori_loop(0, 4, quarter, 0)
 
+    def slab_at(b, l, h):
+        return ((2 * b + l) * his + h) * tall
+
     def put(n, block, first):
         buf = slabs[n]
         width = block.shape[1]
@@ -461,53 +540,73 @@
         while at < first + block.shape[0]:
             which, off = at // share, at % share
             size = min(share - off, first + block.shape[0] - at)
-            buf[which % 2, which // 2, off : off + size, 0:width] = block[at - first : at - first + size].astype(BF16)
+            row = slab_at(which % 2, (which // 2) % 2, which // 4) + off
+            buf[row : row + size, 0:width] = block[at - first : at - first + size].astype(BF16)
             at += size
 
-    def phase_one(n):
-        return remote(slabs[n].at[1 - rbit], recv_a[n], u1s.at[n], u1r.at[n], (2 * ra + 1 - rbit, c))
-
-    def phase_two(n, j):
-        to = (ra + j) % row_a
-        return remote(slabs[n].at[rbit, to], recv_b[n].at[j - 1], u2s.at[n, j - 1], u2r.at[n, j - 1], (2 * to + rbit, c))
+    def one(n):
+        half = 2 * his * tall
+        at = pl.ds(pl.multiple_of((1 - bit) * half, half), half)
+        return remote(slabs[n].at[at, :], recv_a[n], u1s.at[n], u1r.at[n], (r + 1 - 2 * bit, c))
+
+    def two(n):
+        at = pl.ds(pl.multiple_of(slab_at(bit, 1 - lo, 0), his * tall), his * tall)
+        return remote(slabs[n].at[at, :], recv_b[n], u2s.at[n], u2r.at[n], (r + 2 - 4 * lo, c))
+
+    def slab(l, h):
+        return pl.ds(pl.multiple_of(slab_at(bit, l, h), tall), tall)
+
+    def three(n, j):
+        to = (hi + j) % his
+        return remote(
+            slabs[n].at[slab(lo, to), :], recv_c[n].at[j - 1], u3s.at[n, j - 1], u3r.at[n, j - 1],
+            (4 * to + 2 * lo + bit, c),
+        )
+
+    def each_hi(fn):
+        def step(j, carry):
+            fn(j)
+            return carry
+
+        lax.fori_loop(1, his, step, 0)
 
     def start_two(n):
-        phase_one(n).wait_recv()
+        one(n).wait_recv()
 
         def add(i, carry):
-            slabs[n][rbit, i] = (slabs[n][rbit, i].astype(F32) + recv_a[n][i].astype(F32)).astype(BF16)
+            for l in range(2):
+                at = pl.ds(pl.multiple_of((l * his + i) * tall, tall), tall)
+                slabs[n][slab(l, i), :] = (slabs[n][slab(l, i), :].astype(F32) + recv_a[n][at, :].astype(F32)).astype(BF16)
             return carry
 
-        lax.fori_loop(0, row_a, add, 0)
-
-        def send(j, carry):
-            phase_two(n, j).start()
+        lax.fori_loop(0, his, add, 0)
+        two(n).start()
+
+    def start_three(n):
+        two(n).wait_recv()
+
+        def add(i, carry):
+            at = pl.ds(pl.multiple_of(i * tall, tall), tall)
+            slabs[n][slab(lo, i), :] = (slabs[n][slab(lo, i), :].astype(F32) + recv_b[n][at, :].astype(F32)).astype(BF16)
             return carry
 
-        lax.fori_loop(1, row_a, send, 0)
+        lax.fori_loop(0, his, add, 0)
+        each_hi(lambda j: three(n, j).start())
 
     def slab_sent(n):
-        phase_one(n).wait_send()
-
-        def sent(j, carry):
-            phase_two(n, j).wait_send()
-            return carry
-
-        lax.fori_loop(1, row_a, sent, 0)
+        one(n).wait_send()
+        two(n).wait_send()
+        each_hi(lambda j: three(n, j).wait_send())
 
     def col_copy(n, j):
         at = pl.ds(OFFSETS[n], UNITS[n])
         return remote(gath.at[c, :, at], gath.at[c, :, at], ucs.at[n, j - 1], ucr.at[n, j - 1], (r, (c + j) % COLS))
 
     def finish(n):
-        def wait(j, carry):
-            phase_two(n, j).wait_recv()
-            return carry
-
-        lax.fori_loop(1, row_a, wait, 0)
+        each_hi(lambda j: three(n, j).wait_recv())
         gath[c, :, OFFSETS[n] : OFFSETS[n] + UNITS[n]] = (
             lax.fori_loop(
-                0, row_a - 1, lambda j, t: t + recv_b[n][j].astype(F32), slabs[n][rbit, ra].astype(F32)
+                0, his - 1, lambda j, t: t + recv_c[n][j].astype(F32), slabs[n][slab(lo, hi), :].astype(F32)
             )
         ).astype(BF16)
         for j in range(1, COLS):
@@ -515,12 +614,11 @@
 
     for m in range(2):
         put(0, tn(wdn[0:1024, 384 * m : 384 * m + 384], gb[...].reshape(1024, 768)), 384 * m)
-    phase_one(0).start()
+    one(0).start()
     g_dr.forward()
     for m in range(2):
         lanes = jnp.concatenate([a2[b, :, 384 * m : 384 * m + 384] for b in range(4)], axis=0)
         put(1, tn(lanes, wdn[1024:2048, :]), 384 * m)
-    phase_one(1).start()
 
     g_dr.near.wait_recv()
     g_dr.hand.wait_recv()
@@ -531,8 +629,8 @@
         lane = iota((256, 256), 1) & 63
         at = pl.ds(pl.multiple_of(256 * b, 256), 256)
         d_att = nt(drb[b], wop[c]).astype(BF16).astype(F32)
-        attended = jnp.concatenate([att[c, 0, b], att[c, 1, b]], axis=1).astype(F32)
-        rowsum = moved(d_att * attended, bones, 2)
+        mine = jnp.concatenate([att[c, 0, b], att[c, 1, b]], axis=1).astype(F32)
+        rowsum = moved(d_att * mine, bones, 2)
         factor = moved(
             jnp.where(lane == 48, jnp.concatenate([oa[0, at, :], oa[1, at, :]], axis=1), 0.0), bones
         )
@@ -565,49 +663,50 @@
         block = nn(dr_own, both).T
         for h in range(4):
             put(2, block[64 * h : 64 * h + 48], 192 * s + 48 * h)
-    phase_one(2).start()
 
     step_rows = min(rows_n, 8)
     step_keys = 64 * step_rows
 
     def dilated_block(t):
-        tall, wide = pl.multiple_of(64 * (t // 6), 64), pl.multiple_of(512 * (t % 6), 512)
-        return wup.at[pl.ds(tall, 64), pl.ds(wide, 512)]
-
+        tall, wide = pl.multiple_of(64 * (t // 8), 64), pl.multiple_of(384 * (t % 8), 384)
+        return wup.at[pl.ds(tall, 64), pl.ds(wide, 384)]
+
+    d_sel, sums = [], []
     for p in range(2):
-        sides = []
-        for half in range(2):
-            h = 2 * p + half
-            own = (iota((64, 128), 1) >> 6) == half
-            d_sel = jnp.where(own, picked(p, h), 0.0).astype(BF16)
-            sides.append((h, d_sel, picked(2 + p, h)[:, 64 * half : 64 * half + 1]))
-            dqb[h] = jnp.zeros((64, 128), F32)
-
-        def some_keys(n, carry, p=p, sides=sides):
-            some = pl.ds(pl.multiple_of(step_rows * n, step_rows), step_rows)
-            k2 = kvs[some, :, 128 * p : 128 * p + 128].reshape(step_keys, 128)
-            v2 = kvs[some, :, 256 + 128 * p : 384 + 128 * p].reshape(step_keys, 128)
-            dk, dv = 0.0, 0.0
-            for h, d_sel, rs in sides:
-                own = (iota((64, 128), 1) >> 6) == h % 2
-                w = wb[h, :, pl.ds(pl.multiple_of(step_keys * n, step_keys), step_keys)]
-                ds = (w.astype(F32) * (nt(d_sel, v2) - rs)).astype(BF16)
-                dqb[h] += jnp.where(own, nn(ds, k2), 0.0)
-                dk = dk + tn(ds, qsel[h])
-                dv = dv + tn(w, d_sel)
-            for t in range(step_rows):
-                block = dilated_block(step_rows * n + t)
-                block[:, 128 * p : 128 * p + 128] = dk[64 * t : 64 * t + 64].astype(BF16)
-                block[:, 256 + 128 * p : 384 + 128 * p] = dv[64 * t : 64 * t + 64].astype(BF16)
-            return carry
-
-        lax.fori_loop(0, rows_n // step_rows, some_keys, 0)
+        d_sel.append(nn(both_picked(p, p), placing(p, 64)).astype(BF16))
+        sums.append(
+            jnp.concatenate([picked(2 + p, 2 * p + i)[:, 64 * i : 64 * i + 1] for i in range(2)], axis=0)
+        )
+    dqb[...] = jnp.zeros(dqb.shape, F32)
+
+    def some_keys(n, carry):
+        some = pl.ds(pl.multiple_of(step_rows * n, step_rows), step_rows)
+        k2 = kvc[some, :, 0:256].reshape(step_keys, 256)
+        v2 = kvc[some, :, 128:384].reshape(step_keys, 256)
+        dk, dv = 0.0, 0.0
+        for p in range(2):
+            w = wb[p, :, pl.ds(pl.multiple_of(step_keys * n, step_keys), step_keys)]
+            ds = (w.astype(F32) * (nt(d_sel[p], v2) - sums[p])).astype(BF16)
+            dqb[p] += nn(ds, k2)
+            dk = dk + tn(ds, qsel[p])
+            dv = dv + tn(w, d_sel[p])
+        for t in range(step_rows):
+            block = dilated_block(step_rows * n + t)
+            rows = slice(64 * t, 64 * t + 64)
+            block[:, 0:128] = dk[rows, 0:128].astype(BF16)
+            block[:, 128:256] = (dk[rows, 128:256] + dv[rows, 0:128]).astype(BF16)
+            block[:, 256:384] = dv[rows, 128:256].astype(BF16)
+        return carry
+
+    lax.fori_loop(0, rows_n // step_rows, some_keys, 0)
 
     def dilated_copy(j):
         to = (r + j) % rows_n
         return remote(dilated_block(to), dkvr.at[j - 1], bss.at[j - 1], bsr.at[j - 1], (to, c))
 
     each_row(lambda j: dilated_copy(j).start())
+    one(1).start()
+    one(2).start()
 
     qf[...] = jnp.zeros(qf.shape, F32)
 
@@ -617,12 +716,13 @@
     def backward_tile(i):
         h, ib = i // 4, i % 4
         p, half = h // 2, h % 2
-        slot = i % 2
-        weights_in(i).wait()
-
-        @pl.when(i + 1 < 16)
-        def _():
-            weights_in(i + 1).start()
+        slot = i if keep else i % 2
+        if not keep:
+            weights_in(i).wait()
+
+            @pl.when(i + 1 < 16)
+            def _():
+                weights_in(i + 1).start()
 
         rhs = qtm[h, ib]
         for jb in range(4):
@@ -638,19 +738,16 @@
             qf[2 + p, js, :] += jnp.where(own, nn(dsb[js, :], q_rows), 0.0)
             qf[4 + p, js, :] += jnp.where(own, nn(pbuf[slot, js, :], d_rows), 0.0)
 
-    weights_in(0).start()
-    for part in range(4):
-        def bwd(t, carry, part=part):
-            backward_tile(4 * part + t)
+    if not keep:
+        weights_in(0).start()
+    for first, last in ((0, 11), (11, 16)):
+        def bwd(t, carry):
+            backward_tile(t)
             return carry
 
-        lax.fori_loop(0, 4, bwd, 0)
-        if part == 0:
+        lax.fori_loop(first, last, bwd, 0)
+        if first == 0:
             start_two(0)
-        if part == 1:
-            start_two(1)
-        if part == 2:
-            start_two(2)
 
     each_row(lambda j: dilated_copy(j).wait_recv())
     spread = lax.fori_loop(
@@ -660,11 +757,18 @@
     back_qkv = [local(h, wup.at[:, pl.ds(768 * i, 768)], 2 + i) for i, h in enumerate((wq_h, wk_h, wv_h))]
     for d in back_qkv:
         d.start()
+    source, slot = iota((384, 512), 0), iota((384, 512), 1)
+    spread = moved(
+        spread,
+        onehot(((slot & 63) < 48) & (source == 192 * (slot >> 8) + 48 * ((slot & 255) >> 6) + (slot & 63))),
+        2,
+    )
+    dq_b = [moved(dqb[p], placing(p, 0, True), 2) for p in range(2)]
     for h in range(4):
-        p = h // 2
+        p, rows = h // 2, slice(64 * (h % 2), 64 * (h % 2) + 64)
         own = (iota((64, 128), 1) >> 6) == h % 2
         at = pl.ds(LOCAL_HEADS * c + h, 64, stride=STRIDE)
-        qf[p, at, :] += dqb[h]
+        qf[p, at, :] += jnp.where(own, dq_b[p][rows], 0.0)
         qf[2 + p, at, :] += jnp.where(own, spread[:, 128 * p : 128 * p + 128], 0.0)
         qf[4 + p, at, :] += jnp.where(own, spread[:, 256 + 128 * p : 384 + 128 * p], 0.0)
 
@@ -689,9 +793,6 @@
     for j in range(1, COLS):
         exchange(j).start()
     dqr[pl.ds(pl.multiple_of(192 * c, 64), 192), :] = a2[c, 0:192, :]
-    finish(0)
-    finish(1)
-
     rows576 = [
         jnp.concatenate(
             [a2[b, 0:192, 256 * i : 256 * i + 256] for i in range(3)] + [jnp.zeros((64, 256), BF16)], axis=0
@@ -699,14 +800,15 @@
         for b in range(4)
     ]
     lhs = jnp.concatenate(rows576, axis=1)
-    slab_sent(0)
     for m in range(2):
         lanes = jnp.concatenate([a1[b, :, 384 * m : 384 * m + 384] for b in range(4)], axis=0)
         put(3, nn(lhs, lanes).T, 384 * m)
-    phase_one(3).start()
+    one(3).start()
+    start_three(0)
     ones = jnp.ones((16, 1024), BF16)
     vec[7:8, 0:640] = nt(ones, lhs)[0:1]
-    finish(2)
+    start_two(1)
+    finish(0)
 
     for d in back_qkv:
         d.wait()
@@ -719,37 +821,40 @@
     unit, inverse = normalise(tok[c].astype(F32))
     vec[0:1, :] = colsum(da1 * unit)
     vec[1:2, :] = colsum(da1)
-    vec_pair = remote(vec, vpair, vss.at[0], vsr.at[0], (2 * ra + 1 - rbit, c))
-    vec_pair.start()
-    start_two(3)
+    vec_one = remote(vec, vin.at[0], vss.at[0], vsr.at[0], (r + 1 - 2 * bit, c))
+    vec_one.start()
     da2[...] = y1[...] + norm_back(da1, unit, inverse, par[0:1, :])
     gt_copy = local(da2, gt_h, 1)
     gt_copy.start()
-
-    vec_pair.wait_recv()
-    vrow[ra] = vec[...] + vpair[...]
-
-    def vec_copy(j):
-        to = (ra + j) % row_a
-        return remote(vrow.at[ra], vrow.at[ra], vss.at[j], vsr.at[j], (2 * to + rbit, c))
-
-    def each_pair(fn):
-        def step(j, carry):
-            fn(j)
-            return carry
-
-        lax.fori_loop(1, row_a, step, 0)
-
-    each_pair(lambda j: vec_copy(j).start())
-    finish(3)
-    each_pair(lambda j: vec_copy(j).wait_recv())
-    vcol[c] = lax.fori_loop(0, row_a, lambda j, t: t + vrow[j], jnp.zeros((16, 768), F32))
+    start_two(2)
+    vec_one.wait_recv()
+    vcol[c] = vec[...] + vin[0]
+    vec_two = remote(vcol.at[c], vin.at[1], vss.at[1], vsr.at[1], (r + 2 - 4 * lo, c))
+    vec_two.start()
+    start_three(1)
+    start_three(2)
+    vec_two.wait_recv()
+    vrow[hi] = vcol[c] + vin[1]
+
+    def vec_three(j):
+        to = (hi + j) % his
+        return remote(vrow.at[hi], vrow.at[hi], vss.at[1 + j], vsr.at[1 + j], (4 * to + 2 * lo + bit, c))
+
+    each_hi(lambda j: vec_three(j).start())
+    start_two(3)
+    finish(1)
+    finish(2)
+    each_hi(lambda j: vec_three(j).wait_recv())
+    vec_two.wait_send()
+    vcol[c] = lax.fori_loop(0, his, lambda j, t: t + vrow[j], jnp.zeros((16, 768), F32))
 
     def vec_col(j):
         return remote(vcol.at[c], vcol.at[c], vcs.at[j - 1], vcr.at[j - 1], (r, (c + j) % COLS))
 
     for j in range(1, COLS):
         vec_col(j).start()
+    start_three(3)
+    finish(3)
     for j in range(1, COLS):
         vec_col(j).wait_recv()
         for n in range(4):
@@ -759,18 +864,21 @@
     out_gath.start()
     out_vec.start()
 
-    for g in (g_tok, g_cot, *g_att, g_dr):
+    for g in (g_tok, g_cot, g_dr):
         g.drain()
+    for a in attended:
+        for d in (*a.first, *a.rest, *a.hand):
+            d.wait_send()
     each_row(lambda j: sparse_copy(j).wait_send())
-    vec_pair.wait_send()
-    each_pair(lambda j: vec_copy(j).wait_send())
+    vec_one.wait_send()
+    each_hi(lambda j: vec_three(j).wait_send())
     for n in range(4):
-        if n:
-            slab_sent(n)
+        slab_sent(n)
         for j in range(1, COLS):
             col_copy(n, j).wait_send()
     for j in range(1, COLS):
         exchange(j).wait_send()
+        own_dilated(j).wait_send()
         vec_col(j).wait_send()
     out_copy.wait()
     gt_copy.wait()
@@ -778,11 +886,19 @@
     out_vec.wait()
 
 
-def finale(rows_n, gath, vec, out_in, gt_in, out, gt, g1, b1, gq, bq, gk, gv, bv, go, bo, g2, b2, gu, bu, gd, bd):
+def finale(
+    rows_n, gath_h, vec_h, out_h, gt_h, out, gt, g1, b1, gq, bq, gk, gv, bv, go, bo, g2, b2, gu, bu, gd, bd,
+    gath, vec, sems,
+):
+    copies = [
+        pltpu.make_async_copy(src, dst, sems.at[i])
+        for i, (src, dst) in enumerate(((gath_h, gath), (vec_h, vec), (out_h, out), (gt_h, gt)))
+    ]
+    for d in copies:
+        d.start()
     share = 768 // rows_n
     r = lax.axis_index("row")
-    out[...] = out_in[...]
-    gt[...] = gt_in[...]
+    copies[0].wait()
     part = [gath[s].astype(F32)[:share] for s in range(COLS)]
 
     def across(off, width):
@@ -797,6 +913,7 @@
     )
     for s in range(COLS):
         gd[share * s : share * s + share, :] = part[s][:, 0:768]
+    copies[1].wait()
     summed = vec[0] + vec[1] + vec[2] + vec[3]
     wide = max(128, -(-share // 128) * 128)
     f, j = iota((768, wide), 0), iota((768, wide), 1)
@@ -819,24 +936,22 @@
     bq[...] = qv[0][7, :share]
     bv[...] = qv[1][7, :share]
     bu[...] = jnp.concatenate([hidden[s][6:7, :share] for s in range(COLS)], axis=1)[0]
+    copies[2].wait()
+    copies[3].wait()
 
 
 def body(rows_n, tokens, norm1_gain, norm1_bias, w_query, b_query, w_key, w_value, b_value, w_out, b_out,
          norm2_gain, norm2_bias, w_up, b_up, w_down, b_down, slide_padded_units, padding_shortfall, cotangent):
-    row_a, share = rows_n // 2, 768 // rows_n
+    his, share = rows_n // 4, 768 // rows_n
     padded = -(-share // 16) * 16
     c = lax.axis_index("col")
-    par = jnp.concatenate(
-        [
-            jnp.stack([norm1_gain, norm1_bias, b_query, b_value, b_out, norm2_gain, norm2_bias, b_down]),
-            b_up.reshape(4, 768),
-            jnp.zeros((4, 768), F32),
-        ]
-    )
-    down_q = lax.dynamic_index_in_dim(w_down.reshape(rows_n, COLS, share, 768), c, 1, False).reshape(768, 768)
+    down_q = w_down
+    if share % 16:
+        down_q = lax.dynamic_index_in_dim(w_down.reshape(rows_n, COLS, share, 768), c, 1, False).reshape(768, 768)
     vmem = pltpu.VMEM
     dma = pltpu.SemaphoreType.DMA
-    between = max(row_a - 1, 1)
+    between = max(his - 1, 1)
+    keep = rows_n <= 8
     scratch = [
         vmem((768, 3072), BF16), vmem((3072, 768), BF16), vmem((768, 768), BF16), vmem((768, 768), BF16),
         vmem((768, 768), BF16), vmem((4, 256, 768), BF16),
@@ -844,40 +959,43 @@
         vmem((6, 1040, 128), F32), vmem((2, 1024, 128), BF16), vmem((2, 1024, 128), BF16),
         vmem((2, 1024, 128), BF16), vmem((4, 4, 128, 256), BF16), vmem((4, 4, 64, 256), BF16),
         vmem((4, 4, 64, 256), BF16), vmem((4, 4, 8, 256), F32),
-        vmem((2, 1024, 256), BF16), vmem((1024, 256), F32), vmem((1024, 256), BF16),
+        vmem((16 if keep else 2, 1024, 256), BF16), vmem((1024, 256), F32), vmem((1024, 256), BF16),
         vmem((2, 1040, 128), F32), vmem((4, 2, 4, 256, 128), BF16),
         vmem((256, 768), F32), vmem((256, 768), F32), vmem((256, 768), F32),
         vmem((4, 4, 64, 256), F32), vmem((768, 768), BF16),
-        *[vmem((2, row_a, padded, w), BF16) for w in UNITS[:3]],
-        *[vmem((row_a, padded, w), BF16) for w in UNITS],
+        *[vmem((rows_n * padded, w), BF16) for w in UNITS[:3]],
+        *[vmem((2 * his * padded, w), BF16) for w in UNITS],
+        *[vmem((his * padded, w), BF16) for w in UNITS],
         *[vmem((between, padded, w), BF16) for w in UNITS],
         vmem((4, padded, WIDTH), BF16),
-        vmem((rows_n, 64, 512), BF16), vmem((4, 64, 128), BF16), vmem((4, 64, rows_n * 64), BF16),
-        vmem((4, 64, 128), F32), vmem((rows_n - 1, 64, 512), BF16),
-        vmem((16, 768), F32), vmem((16, 768), F32), vmem((row_a, 16, 768), F32), vmem((4, 16, 768), F32), vmem((8, 768), F32),
-        vmem((8, 768), F32),
-        dma((24,)), dma((5, 3)), dma((5, 3)), dma((rows_n - 1,)), dma((rows_n - 1,)), dma((rows_n - 1,)),
-        dma((rows_n - 1,)), dma((4,)), dma((4,)), dma((4, between)), dma((4, between)), dma((4, 3)), dma((4, 3)),
-        dma((3,)), dma((3,)), dma((row_a,)), dma((row_a,)), dma((3,)), dma((3,)), dma((2,)),
+        vmem((4, 16, 384), BF16), vmem((rows_n, 64, 384), BF16), vmem((2, 128, 256), BF16),
+        vmem((2, 128, rows_n * 64), BF16), vmem((2, 128, 256), F32), vmem((rows_n - 1, 64, 384), BF16),
+        vmem((16, 768), F32), vmem((16, 768), F32), vmem((2, 16, 768), F32), vmem((his, 16, 768), F32),
+        vmem((4, 16, 768), F32), vmem((8, 768), F32), vmem((8, 768), F32),
+        dma((24 + rows_n,)), dma((3, 3)), dma((3, 3)), dma((2, 9)), dma((2, 9)), dma((3,)), dma((3,)),
+        dma((rows_n - 1,)), dma((rows_n - 1,)), dma((rows_n - 1,)), dma((rows_n - 1,)),
+        dma((4,)), dma((4,)), dma((4,)), dma((4,)), dma((4, between)), dma((4, between)), dma((4, 3)), dma((4, 3)),
+        dma((3,)), dma((3,)), dma((his + 1,)), dma((his + 1,)), dma((3,)), dma((3,)), dma((2,)),
     ]
     hbm = pl.BlockSpec(memory_space=pl.ANY)
     smem = pl.BlockSpec(memory_space=pltpu.SMEM)
     whole = pl.BlockSpec(memory_space=pltpu.VMEM)
     sds = jax.ShapeDtypeStruct
     out, gt, gath, vec, _ = pl.pallas_call(
-        functools.partial(layer, rows_n, slide_padded_units.shape[0], None),
+        functools.partial(layer, rows_n, slide_padded_units.shape[0], keep),
         out_shape=(
             sds((256, 768), BF16), sds((256, 768), F32), sds((4, padded, WIDTH), BF16), sds((4, 16, 768), F32),
-            sds((16, 1024, 256), BF16),
+            sds((8, 128) if keep else (16, 1024, 256), BF16),
         ),
-        in_specs=[smem, smem, whole] + [hbm] * 9,
+        in_specs=[smem, smem] + [whole] * 9 + [hbm] * 9,
         out_specs=(hbm,) * 5,
         scratch_shapes=scratch,
         compiler_params=pltpu.CompilerParams(
             collective_id=0, has_side_effects=True, vmem_limit_bytes=(992 if rows_n <= 8 else 1021) * 64 * 1024
         ),
         name="layer",
-    )(slide_padded_units, padding_shortfall, par, tokens, cotangent, w_query, w_key, w_value, w_out, w_up, w_down,
+    )(slide_padded_units, padding_shortfall, norm1_gain, norm1_bias, b_query, b_value, b_out, norm2_gain, norm2_bias,
+      b_down, b_up, tokens, cotangent, w_query, w_key, w_value, w_out, w_up, w_down,
       down_q)
     vec1 = sds((share,), F32)
     mat = sds((share, 768), F32)
@@ -887,8 +1005,9 @@
             sds((256, 768), BF16), sds((256, 768), F32), vec1, vec1, mat, vec1, mat, mat, vec1, mat, vec1, vec1, vec1,
             sds((share, 3072), F32), sds((4 * share,), F32), sds((4 * share, 768), F32), vec1,
         ),
-        in_specs=[whole] * 4,
+        in_specs=[hbm] * 4,
         out_specs=(whole,) * 17,
+        scratch_shapes=[vmem((4, padded, WIDTH), BF16), vmem((4, 16, 768), F32), dma((4,))],
         compiler_params=pltpu.CompilerParams(vmem_limit_bytes=48 * 1024 * 1024),
         name="finale",
     )(gath, vec, out, gt)

time: 173 us -> 153 us (0.88)
  local copies, waits for them, and re-layouts: 14.4 us -> 4.56 us
  Pallas kernels: 155 us -> 146 us
    pallas_call x1, Pallas kernels: 152 us -> 142 us  [body(): pl.pallas_call(functools.partial(layer, rows_n, slide_padded_units.shape[...]
    another operation x8 -> x0, local copies, waits for them, and re-layouts: 5.51 us -> none  [body(): jnp.stack([norm1_gain, norm1_bias, b_query, b_value, b_out, norm2_gain, n...]
    dynamic_slice x1 -> x0, local copies, waits for them, and re-layouts: 2.36 us -> none  [body(): lax.dynamic_index_in_dim(w_down.reshape(rows_n, COLS, share, 768), c, 1,...]
where the time goes in v2:
time: 153 us; the launch traced here: 152 us
  Pallas kernels  146 us (95%)
  local copies, waits for them, and re-layouts  4.56 us (3%)
    pallas_call x1, Pallas kernels, body(): pl.pallas_call(functools.partial(layer, rows_n, slide_padded_units.shape[...  142 us
    unnamed x8, local copies, waits for them, and re-layouts  4.56 us
    pallas_call x1, Pallas kernels, body(): pl.pallas_call(functools.partial(finale, rows_n), out_shape=(sds((256, 76...  4.49 us

profile of v2, /device:TPU:0, one launch (start us, length us, event | category | flops | bytes accessed | tf_op | source)
XLA Modules:
  0.0 151.8 jit_solution(784134196852802137)
XLA Ops:
  0.7 141.9 %layer.1 = (bf16[256,768]{1,0:T(8,128)(2,1)}, f32[256,768]{1,0:T(8,128)}, bf16[4,96,2432]{2,1,0:T(8,128)(2,1)}, f32[4,16,768]{2,1,0:T(8,128)}, bf16[8,128]{1,0:T(8,128)(2,1)}) custom-call(s32[8]{0:T(128)} %slide_units.1, s32[8]{0:T(128)} %shortfall.1, f32[768]{0:T(1024)} %v0.1, f32[768]{0:T(1024)} %v1.1, f32[768]{0:T(1024)} %v2.1, f32[768]{0:T(1024)} %v3.1, ...), custom_call_target="tpu_custom_call" | custom-call | tf_op jit(solution)/shard_map/layer/pallas_call | solution.py:984
  142.6 0.0 copy-start
  142.6 1.5 copy-done
  144.1 0.0 copy-start.1
  144.1 1.1 copy-done.1
  145.2 0.0 copy-start.2
  145.2 1.0 copy-done.2
  146.2 0.0 copy-start.3
  146.2 0.9 copy-done.3
  147.1 4.5 %finale.1 = (bf16[256,768]{1,0:T(8,128)(2,1)}, f32[256,768]{1,0:T(8,128)}, f32[96]{0:T(128)}, f32[96]{0:T(128)}, f32[96,768]{1,0:T(8,128)}, /*index=5*/f32[96]{0...) custom-call(bf16[4,96,2432]{2,1,0:T(8,128)(2,1)S(1)} %copy-done, ...), custom_call_target="tpu_custom_call" | custom-call | tf_op jit(solution)/shard_map/finale/pallas_call | solution.py:1002
Async XLA Ops:
  142.6 1.5 copy-start
  144.1 1.1 copy-start.1
  145.2 1.0 copy-start.2
  146.2 0.9 copy-start.3

commit v3 on v2

--- a/solution.py
+++ b/solution.py
@@ -21,8 +21,9 @@
 MESH = pl.DeviceIdType.MESH
 BF16 = jnp.bfloat16
 F32 = jnp.float32
-UNITS = (768, 768, 256, 640)
-OFFSETS = (0, 768, 1536, 1792)
+UNITS = (768, 512, 256, 256, 640)
+OFFSETS = (0, 768, 1280, 1536, 1792)
+DOWN, UP, UP_LAST, OUT, QKV = range(5)
 WIDTH = 2432
 
 
@@ -93,7 +94,7 @@
     qf, qrow, kaug, vaug, qtm, kt, vta, sdr,
     pbuf, sref, dsb, oa, att,
     y1, acc, da2, dqt, dqr,
-    slab0, slab1, slab2, ra0, ra1, ra2, ra3, rb0, rb1, rb2, rb3, rc0, rc1, rc2, rc3, gath,
+    slab0, slab1, slab2, slab3, ra0, ra1, ra2, ra3, ra4, rb0, rb1, rb2, rb3, rb4, rc0, rc1, rc2, rc3, rc4, gath,
     kvo, kvc, qsel, wb, dqb, dkvr,
     par, vec, vin, vrow, vcol, bupq, bqkv,
     lsem, gss, gsr, afs, afr, kos, kor, sps, spr, bss, bsr, u1s, u1r, u2s, u2r, u3s, u3r, ucs, ucr, ats, atr,
@@ -107,8 +108,8 @@
     across = (c + 2) % COLS
     diag = (sib + 2) % COLS
     hi, lo, bit = r // 4, (r // 2) % 2, r % 2
-    recv_a, recv_b, recv_c = (ra0, ra1, ra2, ra3), (rb0, rb1, rb2, rb3), (rc0, rc1, rc2, rc3)
-    slabs = (slab0, slab1, slab2, wdn.at[pl.ds(0, slab0.shape[0]), pl.ds(0, UNITS[3])])
+    recv_a, recv_b, recv_c = (ra0, ra1, ra2, ra3, ra4), (rb0, rb1, rb2, rb3, rb4), (rc0, rc1, rc2, rc3, rc4)
+    slabs = (slab0, slab1, slab2, slab3, wdn.at[pl.ds(0, slab0.shape[0]), pl.ds(0, UNITS[QKV])])
     tall = slab0.shape[0] // rows_n
     key_count = rows_n * 64
 
@@ -117,7 +118,7 @@
 
     in_tok = local(tok_h, tok.at[c], 0)
     in_cot = local(cot_h, gb.at[c], 1)
-    in_qkv = [local(h, wup.at[:, pl.ds(768 * i, 768)], 2 + i) for i, h in enumerate((wq_h, wk_h, wv_h))]
+    in_qkv = [local(h, wdn.at[pl.ds(768 * i, 768), :], 2 + i) for i, h in enumerate((wq_h, wk_h, wv_h))]
     in_up = local(wup_h, wup, 5)
     in_dn = local(wdn_h, wdn, 6)
     if share % 16 == 0:
@@ -146,11 +147,6 @@
         return carry
 
     lax.fori_loop(1, rows_n, greet, 0)
-    for d in in_dq:
-        d.start()
-    for d in in_wo:
-        d.start()
-    in_dn.start()
     pl.semaphore_wait(bar, COLS - 1 + rows_n - 1)
 
     def remote(src, dst, send, recv, dev):
@@ -195,8 +191,6 @@
 
     in_tok.wait()
     g_tok.start()
-    in_cot.wait()
-    g_cot.start()
     for i, v in enumerate((v0, v1, v2, v3, v4, v5, v6, v7)):
         par[i : i + 1, :] = v[...].reshape(1, 768)
     for i in range(4):
@@ -231,7 +225,10 @@
     head_sel = onehot((sel_f == 192 * c + 48 * (sel_j >> 6) + (sel_j & 63)) & ((sel_j & 63) < 48))
     for i, d in enumerate(in_qkv):
         d.wait()
-        wqkv[:, 256 * i : 256 * i + 256] = nn(wup[:, 768 * i : 768 * i + 768], head_sel).astype(BF16)
+        wqkv[:, 256 * i : 256 * i + 256] = nn(wdn[768 * i : 768 * i + 768, :], head_sel).astype(BF16)
+    in_up.start()
+    for d in in_wo:
+        d.start()
     bqkv[...] = jnp.zeros(bqkv.shape, F32)
     biases = moved(par[0:8, :], head_sel)
     bqkv[0:1, 0:256] = biases[2:3]
@@ -247,8 +244,8 @@
     def dilated(values):
         return jnp.sum(jnp.where(on_head, values.astype(BF16).astype(F32), 0.0).reshape(16, 16, 768), axis=1)
 
-    k_sel = dilated(nn(a1[c], wup[:, 768:1536]))
-    v_sel = dilated(nn(a1[c], wup[:, 1536:2304]) + par[3:4, :])
+    k_sel = dilated(nn(a1[c], wdn[768:1536, :]))
+    v_sel = dilated(nn(a1[c], wdn[1536:2304, :]) + par[3:4, :])
     for s in range(COLS):
         kvo[s] = jnp.concatenate(
             [k_sel[:, 192 * s : 192 * s + 192], v_sel[:, 192 * s : 192 * s + 192]], axis=1
@@ -262,7 +259,11 @@
     for j in range(1, COLS):
         own_dilated(j).start()
     kvc[r, own16, :] = kvo[c]
-    in_up.start()
+    in_cot.wait()
+    g_cot.start()
+    in_dn.start()
+    for d in in_dq:
+        d.start()
 
     def qkv_block(b):
         low = a1[b]
@@ -311,23 +312,6 @@
     for j in range(1, COLS):
         own_dilated(j).wait_recv()
     each_row(lambda j: sparse_copy(j).start())
-
-    in_up.wait()
-    for n in range(3):
-        start = (4 * share * ((256 * n) // share)) // 128 * 128
-        stop = -(-(4 * share * ((256 * n + 255) // share + 1)) // 128) * 128
-        o = 256 * n + iota((stop - start, 256), 1)
-        group = jnp.zeros_like(o)
-        for t in range(1, rows_n):
-            group = group + jnp.where(o >= share * t, 1, 0)
-        unit_sel = onehot(start + iota((stop - start, 256), 0) == 3 * share * group + share * c + o)
-        for m in range(3):
-            wupq[256 * m : 256 * m + 256, 256 * n : 256 * n + 256] = nn(
-                wup[256 * m : 256 * m + 256, start:stop], unit_sel
-            ).astype(BF16)
-        pieces = [par[8 + t : 9 + t, :] for t in range(4)]
-        line = jnp.concatenate(pieces, axis=1)[:, start:stop]
-        bupq[0:8, 256 * n : 256 * n + 256] = moved(jnp.broadcast_to(line, (8, stop - start)), unit_sel)
 
     g_tok.forward()
     first_norm(across)
@@ -454,6 +438,24 @@
     for a in attended:
         for d in a.rest:
             d.start()
+
+    in_up.wait()
+    for n in range(3):
+        start = (4 * share * ((256 * n) // share)) // 128 * 128
+        stop = -(-(4 * share * ((256 * n + 255) // share + 1)) // 128) * 128
+        o = 256 * n + iota((stop - start, 256), 1)
+        group = jnp.zeros_like(o)
+        for t in range(1, rows_n):
+            group = group + jnp.where(o >= share * t, 1, 0)
+        unit_sel = onehot(start + iota((stop - start, 256), 0) == 3 * share * group + share * c + o)
+        for m in range(3):
+            wupq[256 * m : 256 * m + 256, 256 * n : 256 * n + 256] = nn(
+                wup[256 * m : 256 * m + 256, start:stop], unit_sel
+            ).astype(BF16)
+        pieces = [par[8 + t : 9 + t, :] for t in range(4)]
+        line = jnp.concatenate(pieces, axis=1)[:, start:stop]
+        bupq[0:8, 256 * n : 256 * n + 256] = moved(jnp.broadcast_to(line, (8, stop - start)), unit_sel)
+
     g_cot.near.wait_recv()
     g_cot.hand.wait_recv()
     vec[5:6, :] = colsum(gb[...].reshape(1024, 768).astype(F32))
@@ -613,12 +615,14 @@
             col_copy(n, j).start()
 
     for m in range(2):
-        put(0, tn(wdn[0:1024, 384 * m : 384 * m + 384], gb[...].reshape(1024, 768)), 384 * m)
-    one(0).start()
+        put(DOWN, tn(wdn[0:1024, 384 * m : 384 * m + 384], gb[...].reshape(1024, 768)), 384 * m)
+    one(DOWN).start()
     g_dr.forward()
     for m in range(2):
         lanes = jnp.concatenate([a2[b, :, 384 * m : 384 * m + 384] for b in range(4)], axis=0)
-        put(1, tn(lanes, wdn[1024:2048, :]), 384 * m)
+        block = tn(lanes, wdn[1024:2048, :])
+        put(UP, block[:, 0:512], 384 * m)
+        put(UP_LAST, block[:, 512:768], 384 * m)
 
     g_dr.near.wait_recv()
     g_dr.hand.wait_recv()
@@ -662,7 +666,7 @@
         )
         block = nn(dr_own, both).T
         for h in range(4):
-            put(2, block[64 * h : 64 * h + 48], 192 * s + 48 * h)
+            put(OUT, block[64 * h : 64 * h + 48], 192 * s + 48 * h)
 
     step_rows = min(rows_n, 8)
     step_keys = 64 * step_rows
@@ -705,8 +709,6 @@
         return remote(dilated_block(to), dkvr.at[j - 1], bss.at[j - 1], bsr.at[j - 1], (to, c))
 
     each_row(lambda j: dilated_copy(j).start())
-    one(1).start()
-    one(2).start()
 
     qf[...] = jnp.zeros(qf.shape, F32)
 
@@ -747,7 +749,9 @@
 
         lax.fori_loop(first, last, bwd, 0)
         if first == 0:
-            start_two(0)
+            start_two(DOWN)
+            one(UP).start()
+            one(OUT).start()
 
     each_row(lambda j: dilated_copy(j).wait_recv())
     spread = lax.fori_loop(
@@ -802,13 +806,15 @@
     lhs = jnp.concatenate(rows576, axis=1)
     for m in range(2):
         lanes = jnp.concatenate([a1[b, :, 384 * m : 384 * m + 384] for b in range(4)], axis=0)
-        put(3, nn(lhs, lanes).T, 384 * m)
-    one(3).start()
-    start_three(0)
+        put(QKV, nn(lhs, lanes).T, 384 * m)
+    one(QKV).start()
+    start_three(DOWN)
     ones = jnp.ones((16, 1024), BF16)
     vec[7:8, 0:640] = nt(ones, lhs)[0:1]
-    start_two(1)
-    finish(0)
+    start_two(UP)
+    start_two(OUT)
+    finish(DOWN)
+    start_three(UP)
 
     for d in back_qkv:
         d.wait()
@@ -826,13 +832,15 @@
     da2[...] = y1[...] + norm_back(da1, unit, inverse, par[0:1, :])
     gt_copy = local(da2, gt_h, 1)
     gt_copy.start()
-    start_two(2)
+    start_two(QKV)
+    one(UP_LAST).start()
+    start_three(OUT)
     vec_one.wait_recv()
     vcol[c] = vec[...] + vin[0]
     vec_two = remote(vcol.at[c], vin.at[1], vss.at[1], vsr.at[1], (r + 2 - 4 * lo, c))
     vec_two.start()
-    start_three(1)
-    start_three(2)
+    finish(UP)
+    start_two(UP_LAST)
     vec_two.wait_recv()
     vrow[hi] = vcol[c] + vin[1]
 
@@ -841,9 +849,9 @@
         return remote(vrow.at[hi], vrow.at[hi], vss.at[1 + j], vsr.at[1 + j], (4 * to + 2 * lo + bit, c))
 
     each_hi(lambda j: vec_three(j).start())
-    start_two(3)
-    finish(1)
-    finish(2)
+    finish(OUT)
+    start_three(QKV)
+    start_three(UP_LAST)
     each_hi(lambda j: vec_three(j).wait_recv())
     vec_two.wait_send()
     vcol[c] = lax.fori_loop(0, his, lambda j, t: t + vrow[j], jnp.zeros((16, 768), F32))
@@ -853,11 +861,11 @@
 
     for j in range(1, COLS):
         vec_col(j).start()
-    start_three(3)
-    finish(3)
+    finish(QKV)
+    finish(UP_LAST)
     for j in range(1, COLS):
         vec_col(j).wait_recv()
-        for n in range(4):
+        for n in range(5):
             col_copy(n, j).wait_recv()
     out_gath = local(gath, gath_h, 2)
     out_vec = local(vcol, vec_h, 3)
@@ -872,7 +880,7 @@
     each_row(lambda j: sparse_copy(j).wait_send())
     vec_one.wait_send()
     each_hi(lambda j: vec_three(j).wait_send())
-    for n in range(4):
+    for n in range(5):
         slab_sent(n)
         for j in range(1, COLS):
             col_copy(n, j).wait_send()
@@ -963,7 +971,7 @@
         vmem((2, 1040, 128), F32), vmem((4, 2, 4, 256, 128), BF16),
         vmem((256, 768), F32), vmem((256, 768), F32), vmem((256, 768), F32),
         vmem((4, 4, 64, 256), F32), vmem((768, 768), BF16),
-        *[vmem((rows_n * padded, w), BF16) for w in UNITS[:3]],
+        *[vmem((rows_n * padded, w), BF16) for w in UNITS[:QKV]],
         *[vmem((2 * his * padded, w), BF16) for w in UNITS],
         *[vmem((his * padded, w), BF16) for w in UNITS],
         *[vmem((between, padded, w), BF16) for w in UNITS],
@@ -974,7 +982,7 @@
         vmem((4, 16, 768), F32), vmem((8, 768), F32), vmem((8, 768), F32),
         dma((24 + rows_n,)), dma((3, 3)), dma((3, 3)), dma((2, 9)), dma((2, 9)), dma((3,)), dma((3,)),
         dma((rows_n - 1,)), dma((rows_n - 1,)), dma((rows_n - 1,)), dma((rows_n - 1,)),
-        dma((4,)), dma((4,)), dma((4,)), dma((4,)), dma((4, between)), dma((4, between)), dma((4, 3)), dma((4, 3)),
+        dma((5,)), dma((5,)), dma((5,)), dma((5,)), dma((5, between)), dma((5, between)), dma((5, 3)), dma((5, 3)),
         dma((3,)), dma((3,)), dma((his + 1,)), dma((his + 1,)), dma((3,)), dma((3,)), dma((2,)),
     ]
     hbm = pl.BlockSpec(memory_space=pl.ANY)
@@ -1005,10 +1013,10 @@
             sds((256, 768), BF16), sds((256, 768), F32), vec1, vec1, mat, vec1, mat, mat, vec1, mat, vec1, vec1, vec1,
             sds((share, 3072), F32), sds((4 * share,), F32), sds((4 * share, 768), F32), vec1,
         ),
-        in_specs=[hbm] * 4,
+        in_specs=[pl.BlockSpec(memory_space=pltpu.HBM)] * 4,
         out_specs=(whole,) * 17,
         scratch_shapes=[vmem((4, padded, WIDTH), BF16), vmem((4, 16, 768), F32), dma((4,))],
-        compiler_params=pltpu.CompilerParams(vmem_limit_bytes=48 * 1024 * 1024),
+        compiler_params=pltpu.CompilerParams(vmem_limit_bytes=1016 * 64 * 1024),
         name="finale",
     )(gath, vec, out, gt)
 

time: 153 us -> 137 us (0.90)
  Pallas kernels: 146 us -> 135 us
  local copies, waits for them, and re-layouts: 4.56 us -> 0 us
    pallas_call x1, Pallas kernels: 142 us -> 130 us  [body(): pl.pallas_call(functools.partial(layer, rows_n, slide_padded_units.shape[...]
    unnamed x8 -> x0, local copies, waits for them, and re-layouts: 4.56 us -> none
where the time goes in v3:
time: 137 us; the launch traced here: 136 us
  Pallas kernels  135 us (99%)
    pallas_call x1, Pallas kernels, body(): pl.pallas_call(functools.partial(layer, rows_n, slide_padded_units.shape[...  130 us
    pallas_call x1, Pallas kernels, body(): pl.pallas_call(functools.partial(finale, rows_n), out_shape=(sds((256, 76...  5.26 us

profile of v3, /device:TPU:0, one launch (start us, length us, event | category | flops | bytes accessed | tf_op | source)
XLA Modules:
  0.0 136.0 jit_solution(4184479841548470190)
XLA Ops:
  0.7 129.9 %layer.1 = (bf16[256,768]{1,0:T(8,128)(2,1)}, f32[256,768]{1,0:T(8,128)}, bf16[4,96,2432]{2,1,0:T(8,128)(2,1)}, f32[4,16,768]{2,1,0:T(8,128)}, bf16[8,128]{1,0:T(8,128)(2,1)}) custom-call(s32[8]{0:T(128)} %slide_units.1, s32[8]{0:T(128)} %shortfall.1, f32[768]{0:T(1024)} %v0.1, f32[768]{0:T(1024)} %v1.1, f32[768]{0:T(1024)} %v2.1, f32[768]{0:T(1024)} %v3.1, ...), custom_call_target="tpu_custom_call" | custom-call | tf_op jit(solution)/shard_map/layer/pallas_call | solution.py:992
  130.6 5.3 %finale.1 = (bf16[256,768]{1,0:T(8,128)(2,1)}, f32[256,768]{1,0:T(8,128)}, f32[96]{0:T(128)}, f32[96]{0:T(128)}, f32[96,768]{1,0:T(8,128)}, /*index=5*/f32[96]{0...) custom-call(bf16[4,96,2432]{2,1,0:T(8,128)(2,1)} %get-tuple-element., ...), custom_call_target="tpu_custom_call" | custom-call | tf_op jit(solution)/shard_map/finale/pallas_call | solution.py:1010

commit v4 on v3

--- a/solution.py
+++ b/solution.py
@@ -21,9 +21,9 @@
 MESH = pl.DeviceIdType.MESH
 BF16 = jnp.bfloat16
 F32 = jnp.float32
-UNITS = (768, 512, 256, 256, 640)
-OFFSETS = (0, 768, 1280, 1536, 1792)
-DOWN, UP, UP_LAST, OUT, QKV = range(5)
+UNITS = (768, 512, 256, 256, 384, 256)
+OFFSETS = (0, 768, 1280, 1536, 1792, 2176)
+DOWN, UP, UP_LAST, OUT, QK, VAL = range(6)
 WIDTH = 2432
 
 
@@ -94,7 +94,7 @@
     qf, qrow, kaug, vaug, qtm, kt, vta, sdr,
     pbuf, sref, dsb, oa, att,
     y1, acc, da2, dqt, dqr,
-    slab0, slab1, slab2, slab3, ra0, ra1, ra2, ra3, ra4, rb0, rb1, rb2, rb3, rb4, rc0, rc1, rc2, rc3, rc4, gath,
+    slab0, slab1, slab2, slab3, ra0, ra1, ra2, ra3, ra4, ra5, rb0, rb1, rb2, rb3, rb4, rb5, rc0, rc1, rc2, rc3, rc4, rc5, gath,
     kvo, kvc, qsel, wb, dqb, dkvr,
     par, vec, vin, vrow, vcol, bupq, bqkv,
     lsem, gss, gsr, afs, afr, kos, kor, sps, spr, bss, bsr, u1s, u1r, u2s, u2r, u3s, u3r, ucs, ucr, ats, atr,
@@ -108,8 +108,12 @@
     across = (c + 2) % COLS
     diag = (sib + 2) % COLS
     hi, lo, bit = r // 4, (r // 2) % 2, r % 2
-    recv_a, recv_b, recv_c = (ra0, ra1, ra2, ra3, ra4), (rb0, rb1, rb2, rb3, rb4), (rc0, rc1, rc2, rc3, rc4)
-    slabs = (slab0, slab1, slab2, slab3, wdn.at[pl.ds(0, slab0.shape[0]), pl.ds(0, UNITS[QKV])])
+    recv_a, recv_b, recv_c = (ra0, ra1, ra2, ra3, ra4, ra5), (rb0, rb1, rb2, rb3, rb4, rb5), (rc0, rc1, rc2, rc3, rc4, rc5)
+    slabs = (
+        slab0, slab1, slab2, slab3,
+        wdn.at[pl.ds(0, slab0.shape[0]), pl.ds(0, UNITS[QK])],
+        wdn.at[pl.ds(0, slab0.shape[0]), pl.ds(UNITS[QK], UNITS[VAL])],
+    )
     tall = slab0.shape[0] // rows_n
     key_count = rows_n * 64
 
@@ -748,6 +752,8 @@
             return carry
 
         lax.fori_loop(first, last, bwd, 0)
+        if first:
+            one(UP_LAST).start()
         if first == 0:
             start_two(DOWN)
             one(UP).start()
@@ -804,17 +810,24 @@
         for b in range(4)
     ]
     lhs = jnp.concatenate(rows576, axis=1)
-    for m in range(2):
-        lanes = jnp.concatenate([a1[b, :, 384 * m : 384 * m + 384] for b in range(4)], axis=0)
-        put(QKV, nn(lhs, lanes).T, 384 * m)
-    one(QKV).start()
-    start_three(DOWN)
+    def own_grads(n, first):
+        for m in range(2):
+            lanes = jnp.concatenate([a1[b, :, 384 * m : 384 * m + 384] for b in range(4)], axis=0)
+            put(n, nn(lhs[first : first + UNITS[n]], lanes).T, 384 * m)
+
+    own_grads(QK, 0)
+    one(QK).start()
+    own_grads(VAL, UNITS[QK])
     ones = jnp.ones((16, 1024), BF16)
     vec[7:8, 0:640] = nt(ones, lhs)[0:1]
+    start_three(DOWN)
     start_two(UP)
     start_two(OUT)
+    start_two(UP_LAST)
     finish(DOWN)
     start_three(UP)
+    start_two(QK)
+    one(VAL).start()
 
     for d in back_qkv:
         d.wait()
@@ -832,15 +845,16 @@
     da2[...] = y1[...] + norm_back(da1, unit, inverse, par[0:1, :])
     gt_copy = local(da2, gt_h, 1)
     gt_copy.start()
-    start_two(QKV)
-    one(UP_LAST).start()
     start_three(OUT)
+    start_three(UP_LAST)
+    start_two(VAL)
+    start_three(QK)
     vec_one.wait_recv()
     vcol[c] = vec[...] + vin[0]
     vec_two = remote(vcol.at[c], vin.at[1], vss.at[1], vsr.at[1], (r + 2 - 4 * lo, c))
     vec_two.start()
     finish(UP)
-    start_two(UP_LAST)
+    finish(OUT)
     vec_two.wait_recv()
     vrow[hi] = vcol[c] + vin[1]
 
@@ -849,9 +863,8 @@
         return remote(vrow.at[hi], vrow.at[hi], vss.at[1 + j], vsr.at[1 + j], (4 * to + 2 * lo + bit, c))
 
     each_hi(lambda j: vec_three(j).start())
-    finish(OUT)
-    start_three(QKV)
-    start_three(UP_LAST)
+    finish(UP_LAST)
+    start_three(VAL)
     each_hi(lambda j: vec_three(j).wait_recv())
     vec_two.wait_send()
     vcol[c] = lax.fori_loop(0, his, lambda j, t: t + vrow[j], jnp.zeros((16, 768), F32))
@@ -861,11 +874,11 @@
 
     for j in range(1, COLS):
         vec_col(j).start()
-    finish(QKV)
-    finish(UP_LAST)
+    finish(QK)
+    finish(VAL)
     for j in range(1, COLS):
         vec_col(j).wait_recv()
-        for n in range(5):
+        for n in range(6):
             col_copy(n, j).wait_recv()
     out_gath = local(gath, gath_h, 2)
     out_vec = local(vcol, vec_h, 3)
@@ -880,7 +893,7 @@
     each_row(lambda j: sparse_copy(j).wait_send())
     vec_one.wait_send()
     each_hi(lambda j: vec_three(j).wait_send())
-    for n in range(5):
+    for n in range(6):
         slab_sent(n)
         for j in range(1, COLS):
             col_copy(n, j).wait_send()
@@ -971,7 +984,7 @@
         vmem((2, 1040, 128), F32), vmem((4, 2, 4, 256, 128), BF16),
         vmem((256, 768), F32), vmem((256, 768), F32), vmem((256, 768), F32),
         vmem((4, 4, 64, 256), F32), vmem((768, 768), BF16),
-        *[vmem((rows_n * padded, w), BF16) for w in UNITS[:QKV]],
+        *[vmem((rows_n * padded, w), BF16) for w in UNITS[:QK]],
         *[vmem((2 * his * padded, w), BF16) for w in UNITS],
         *[vmem((his * padded, w), BF16) for w in UNITS],
         *[vmem((between, padded, w), BF16) for w in UNITS],
@@ -982,7 +995,7 @@
         vmem((4, 16, 768), F32), vmem((8, 768), F32), vmem((8, 768), F32),
         dma((24 + rows_n,)), dma((3, 3)), dma((3, 3)), dma((2, 9)), dma((2, 9)), dma((3,)), dma((3,)),
         dma((rows_n - 1,)), dma((rows_n - 1,)), dma((rows_n - 1,)), dma((rows_n - 1,)),
-        dma((5,)), dma((5,)), dma((5,)), dma((5,)), dma((5, between)), dma((5, between)), dma((5, 3)), dma((5, 3)),
+        dma((6,)), dma((6,)), dma((6,)), dma((6,)), dma((6, between)), dma((6, between)), dma((6, 3)), dma((6, 3)),
         dma((3,)), dma((3,)), dma((his + 1,)), dma((his + 1,)), dma((3,)), dma((3,)), dma((2,)),
     ]
     hbm = pl.BlockSpec(memory_space=pl.ANY)

time: 137 us -> 134 us (0.978)
  Pallas kernels: 135 us -> 133 us
    pallas_call x1, Pallas kernels: 130 us -> 127 us  [body(): pl.pallas_call(functools.partial(layer, rows_n, slide_padded_units.shape[...]
where the time goes in v4:
time: 134 us
  Pallas kernels  133 us (99%)
    pallas_call x1, Pallas kernels, body(): pl.pallas_call(functools.partial(layer, rows_n, slide_padded_units.shape[...  127 us
    pallas_call x1, Pallas kernels, body(): pl.pallas_call(functools.partial(finale, rows_n), out_shape=(sds((256, 76...  5.26 us

profile of v4, /device:TPU:0, one launch (start us, length us, event | category | flops | bytes accessed | tf_op | source)
XLA Modules:
  0.0 133.5 jit_solution(6578588114434175084)
XLA Ops:
  0.7 127.4 %layer.1 = (bf16[256,768]{1,0:T(8,128)(2,1)}, f32[256,768]{1,0:T(8,128)}, bf16[4,96,2432]{2,1,0:T(8,128)(2,1)}, f32[4,16,768]{2,1,0:T(8,128)}, bf16[8,128]{1,0:T(8,128)(2,1)}) custom-call(s32[8]{0:T(128)} %slide_units.1, s32[8]{0:T(128)} %shortfall.1, f32[768]{0:T(1024)} %v0.1, f32[768]{0:T(1024)} %v1.1, f32[768]{0:T(1024)} %v2.1, f32[768]{0:T(1024)} %v3.1, ...), custom_call_target="tpu_custom_call" | custom-call | tf_op jit(solution)/shard_map/layer/pallas_call | solution.py:1005
  128.1 5.3 %finale.1 = (bf16[256,768]{1,0:T(8,128)(2,1)}, f32[256,768]{1,0:T(8,128)}, f32[96]{0:T(128)}, f32[96]{0:T(128)}, f32[96,768]{1,0:T(8,128)}, /*index=5*/f32[96]{0...) custom-call(bf16[4,96,2432]{2,1,0:T(8,128)(2,1)} %get-tuple-element., ...), custom_call_target="tpu_custom_call" | custom-call | tf_op jit(solution)/shard_map/finale/pallas_call | solution.py:1023

commit v5 on v4

--- a/solution.py
+++ b/solution.py
@@ -753,7 +753,7 @@
 
         lax.fori_loop(first, last, bwd, 0)
         if first:
-            one(UP_LAST).start()
+            start_three(DOWN)
         if first == 0:
             start_two(DOWN)
             one(UP).start()
@@ -820,14 +820,14 @@
     own_grads(VAL, UNITS[QK])
     ones = jnp.ones((16, 1024), BF16)
     vec[7:8, 0:640] = nt(ones, lhs)[0:1]
-    start_three(DOWN)
     start_two(UP)
     start_two(OUT)
-    start_two(UP_LAST)
+    one(UP_LAST).start()
     finish(DOWN)
     start_three(UP)
     start_two(QK)
     one(VAL).start()
+    start_two(UP_LAST)
 
     for d in back_qkv:
         d.wait()

time: 134 us -> 134 us (level)
  no operation moved by 1% of the time
where the time goes in v5:
time: 134 us
  Pallas kernels  133 us (99%)
    pallas_call x1, Pallas kernels, body(): pl.pallas_call(functools.partial(layer, rows_n, slide_padded_units.shape[...  128 us
    pallas_call x1, Pallas kernels, body(): pl.pallas_call(functools.partial(finale, rows_n), out_shape=(sds((256, 76...  5.26 us

profile of v5, /device:TPU:0, one launch (start us, length us, event | category | flops | bytes accessed | tf_op | source)
XLA Modules:
  0.0 134.0 jit_solution(8941832338281931986)
XLA Ops:
  0.7 127.9 %layer.1 = (bf16[256,768]{1,0:T(8,128)(2,1)}, f32[256,768]{1,0:T(8,128)}, bf16[4,96,2432]{2,1,0:T(8,128)(2,1)}, f32[4,16,768]{2,1,0:T(8,128)}, bf16[8,128]{1,0:T(8,128)(2,1)}) custom-call(s32[8]{0:T(128)} %slide_units.1, s32[8]{0:T(128)} %shortfall.1, f32[768]{0:T(1024)} %v0.1, f32[768]{0:T(1024)} %v1.1, f32[768]{0:T(1024)} %v2.1, f32[768]{0:T(1024)} %v3.1, ...), custom_call_target="tpu_custom_call" | custom-call | tf_op jit(solution)/shard_map/layer/pallas_call | solution.py:1005
  128.6 5.3 %finale.1 = (bf16[256,768]{1,0:T(8,128)(2,1)}, f32[256,768]{1,0:T(8,128)}, f32[96]{0:T(128)}, f32[96]{0:T(128)}, f32[96,768]{1,0:T(8,128)}, /*index=5*/f32[96]{0...) custom-call(bf16[4,96,2432]{2,1,0:T(8,128)(2,1)} %get-tuple-element., ...), custom_call_target="tpu_custom_call" | custom-call | tf_op jit(solution)/shard_map/finale/pallas_call | solution.py:1023
